TPU v7x, 32 devices: a whole 2x2x4 slice. The times are simulated.
32 devices in a mesh: date: 4 (over y, core), strip: 8 (over z, x).
Axes of the slice: x: 2, y: 2, z: 4, core: 2. Of those that a mesh axis runs over, the one named last changes fastest.
Arguments:
- stack: float32 [64, 512, 1024], P('date', 'strip'), may hold values from -6 to 6
- spatial_taps: float32 [13], replicated, may hold values from 0.2 to 1
- temporal_taps: float32 [2, 5], replicated, may hold values from -0.25 to 0.25
- foot_tile: int32 [1024], P(('date', 'strip')), may hold values from 0 to 1
- foot_row: int32 [1024], P(('date', 'strip')), may hold values from 0 to 63
- foot_count: int32 [1024], P(('date', 'strip')), may hold values from 1 to 128
- foot_owner: int32 [1024, 1], P(('date', 'strip')), may hold values from 0 to 31; in each aligned block of 32 rows (0 to 31, 32 to 63, ...) at most 2 rows name the same one
Outputs:
- residual: float32 [64, 512, 1024], P(None, 'strip', 'date')
- anomaly: float32 [32, 64, 64], P(('date', 'strip'))
- asset_series: float32 [32, 64], P(('date', 'strip'))
Inputs may be any that keep to these rules, and one draw needn't show every extreme that they name: `foot_owner`: among the footprints of one block, no owner appears more than 2 times, a bound that some block reaches; every owner has some footprint.
All inputs are finite; a program needn't handle non-finite values.
Results may differ from a plain program's by a relative error of at most 0.000075.
Values sent between devices are 32-bit elements; how exact they have to be, the bound alone decides.
No kernel may reach another device: no remote copies, remote signals or barrier semaphores. Data moves between devices by JAX's collectives and lax.ppermute only.
A program may use at most 128 MiB of HBM per device.

v0:
```python
import functools

import jax
import jax.numpy as jnp
from jax import lax
from jax.experimental import pallas as pl
from jax.experimental.pallas import tpu as pltpu
from jax.sharding import PartitionSpec as P

TILE = 128
RADIUS = 6
REACH = 2
DILATION = 8
PAIR_CAP = 2
LANES = 128
EDGE = 8
HIGHEST = lax.Precision.HIGHEST


def params(mebibytes):
    return pltpu.CompilerParams(vmem_limit_bytes=mebibytes * 1024 * 1024)


def cost(micros):
    return pl.CostEstimate(flops=0, bytes_accessed=int(micros * 3.69e6), transcendentals=0)


def pick_taps(at, taps):
    count = taps.shape[0]
    total = taps[0]
    for k in range(1, count):
        total = total + taps[k]
    out = jnp.zeros(at.shape, jnp.float32)
    for k in range(count):
        out = jnp.where(at == k, taps[k], out)
    return out / jnp.full(at.shape, total, jnp.float32)


def split(value, count):
    out = []
    for _ in range(count):
        piece = value.astype(jnp.bfloat16)
        out.append(piece)
        value = value - piece.astype(jnp.float32)
    return out


def spread(value, axis):
    high, mid = split(value, 2)
    return jnp.concatenate([high, high, high, mid], axis=axis)


def fill_columns(col_ref, taps):
    shape = (LANES, LANES)
    lag = lax.broadcasted_iota(jnp.int32, shape, 0) - lax.broadcasted_iota(jnp.int32, shape, 1)
    near = split(pick_taps(lag + RADIUS, taps), 3)
    far = pick_taps(jnp.where(lag > 0, lag + RADIUS - LANES, lag + RADIUS + LANES), taps)
    above = split(jnp.where(lag > 0, far, 0.0), 3)
    below = split(jnp.where(lag > 0, 0.0, far), 3)
    for n, piece in enumerate((0, 1, 2, 0)):
        at = n * 3 * LANES
        for i, pair in enumerate(((near, above), (below, near), (above, below))):
            for j, block in enumerate(pair):
                col_ref[at + i * LANES:at + (i + 1) * LANES, j * LANES:(j + 1) * LANES] = block[piece]


def row_band(out_rows, in_rows, taps):
    shape = (out_rows, 4 * in_rows)
    lane = lax.broadcasted_iota(jnp.int32, shape, 1)
    row = lax.broadcasted_iota(jnp.int32, shape, 0)
    part = jnp.zeros(shape, jnp.int32)
    for n in range(1, 4):
        part = jnp.where(lane >= n * in_rows, n, part)
    return lane - part * in_rows, row, part


def pieces_of(values, part):
    high, mid, low = [p.astype(jnp.float32) for p in split(values, 3)]
    return jnp.where(part == 1, mid, jnp.where(part == 2, low, high)).astype(jnp.bfloat16)


def filter_columns(mid, rim, col):
    rows = mid.shape[0]
    window = jnp.concatenate([mid, rim], axis=1)
    return jnp.dot(spread(window, 1), col, preferred_element_type=jnp.float32)


def rim_tile(left, right, block, parts):
    lane = lax.broadcasted_iota(jnp.int32, left.shape, len(left.shape) - 1)
    first = lane < LANES // 2
    keep = (first & (block < parts - 1)) | (~first & (block > 0))
    return jnp.where(keep, jnp.where(first, right, left), 0.0)


def chosen(n, values):
    out = values[0]
    for m in range(1, len(values)):
        out = jnp.where(n == m, values[m], out)
    return out


def interior_kernel(offsets, slot, parts, group, place, taps, stack, *rest):
    count = len(offsets)
    first = slot == 0
    if not first:
        rest = rest[1:]
    outs, brim, rest = rest[:count], rest[count], rest[count + 1:]
    if first:
        up, down, ends, mid_ref, left_ref, right_ref, halo_ref, up_ref, down_ref, halo_sem, halo_out_sem, *rest = rest
    else:
        x_ref, *rest = rest
    out_ref, brim_ref, col_ref, row_ref, in_sem, out_sem, brim_sem = rest
    _, per, dates, inner, _ = out_ref.shape
    width = per * LANES
    rows = inner + 2 * EDGE
    cols = width * parts
    steps = dates // group

    def bounds(block):
        start = block * width
        places = start, jnp.maximum(start - LANES, 0), jnp.minimum(start + width, cols - LANES)
        return [pl.multiple_of(at, LANES) for at in places]

    def load(g):
        at = pl.ds(g * group, group)
        if not first:
            return [pltpu.make_async_copy(stack.at[at], x_ref.at[at], in_sem.at[0, g])]
        return [
            pltpu.make_async_copy(stack.at[at, :, pl.ds(start, ref.shape[2])], ref.at[at], in_sem.at[n, g])
            for n, (start, ref) in enumerate(zip(bounds(place[0] ^ offsets[0]), (mid_ref, left_ref, right_ref)))
        ]

    def store(m, g):
        at = pl.ds(g * group, group)
        return pltpu.make_async_copy(out_ref.at[m, :, at], outs[m].at[:, at], out_sem.at[m, g])

    def store_brim(n):
        return pltpu.make_async_copy(brim_ref.at[n], brim.at[slot + n], brim_sem.at[n])

    for g in range(steps):
        for copy in load(g):
            copy.start()
    halo_loads, halo_stores = [], []
    if first:
        halo_loads = [
            pltpu.make_async_copy(
                stack.at[:, pl.ds(side * (rows - EDGE), EDGE), pl.ds(c * LANES, LANES)],
                halo_ref.at[c, :, pl.ds(side * EDGE, EDGE), :], halo_sem.at[side, c])
            for side in range(2) for c in range(cols // LANES)
        ]
        halo_stores = [
            pltpu.make_async_copy(halo_ref, ends, halo_out_sem.at[0]),
            pltpu.make_async_copy(up_ref, up, halo_out_sem.at[1]),
            pltpu.make_async_copy(down_ref, down, halo_out_sem.at[2]),
        ]
        for copy in halo_loads:
            copy.start()
    fill_columns(col_ref, taps)
    q, r, part = row_band(inner, rows, taps)
    row_ref[...] = pieces_of(pick_taps(q - r - (EDGE - RADIUS), taps), part)

    def pack(c, carry):
        at = pl.ds(pl.multiple_of(c * LANES, LANES), LANES)
        rows_of = halo_ref.at[c].reshape(dates * 2 * EDGE, LANES)
        for r in range(RADIUS):
            up_ref[r, :, at] = rows_of[pl.ds(2 * EDGE - RADIUS + r, dates, stride=2 * EDGE), :]
            down_ref[r, :, at] = rows_of[pl.ds(r, dates, stride=2 * EDGE), :]
        return carry

    def step(i, carry):
        n, g = i // steps, i % steps
        block = place[0] ^ chosen(n, offsets)
        at = pl.ds(g * group, group)

        @pl.when(n == 0)
        def _():
            for copy in load(g):
                copy.wait()

        if first:
            @pl.when(i == steps - 1)
            def _():
                for copy in halo_loads:
                    copy.wait()
                lax.fori_loop(0, cols // LANES, pack, 0)
                for copy in halo_stores:
                    copy.start()

            mid, left, right = mid_ref[at], left_ref[at], right_ref[at]
        else:
            start, before, after = bounds(block)
            mid, left, right = [x_ref[at, :, pl.ds(f, w)] for f, w in ((start, width), (before, LANES), (after, LANES))]
        rim = rim_tile(left, right, block, parts)
        across = filter_columns(mid.reshape(group * rows, width), rim.reshape(group * rows, LANES), col_ref[...])
        for t in range(group):
            one = across[t * rows:(t + 1) * rows]
            low = jnp.dot(row_ref[...], spread(one, 0), preferred_element_type=jnp.float32)
            done = mid[t, EDGE:rows - EDGE, :] - low
            for h in range(per):
                out_ref[n, h, g * group + t] = done[:, h * LANES:(h + 1) * LANES]
                for side in range(2):
                    lines = one[side * (rows - 2 * EDGE):side * (rows - 2 * EDGE) + 2 * EDGE, h * LANES:(h + 1) * LANES]
                    date = g * group + t
                    at = ((date // EDGE) * 4 * EDGE + side * 2 * EDGE) * EDGE + date % EDGE
                    brim_ref[n, h, pl.ds(at, 2 * EDGE, stride=EDGE), :] = lines
        for m in range(count):
            @pl.when(n == m)
            def _():
                store(m, g).start()

        @pl.when(g == steps - 1)
        def _():
            store_brim(n).start()

        return carry

    lax.fori_loop(0, count * steps, step, 0)
    for copy in halo_stores:
        copy.wait()
    for m in range(count):
        for g in range(steps):
            store(m, g).wait()
        store_brim(m).wait()


def interior(stack, brim, taps, place, offsets, slot, parts):
    dates, rows, cols = stack.shape
    width = cols // parts
    per = width // LANES
    group = min(8, dates)
    inner = rows - 2 * EDGE
    count = len(offsets)
    first = slot == 0
    here = pl.BlockSpec(memory_space=pltpu.HBM)
    out_shape = [jax.ShapeDtypeStruct((per, dates, inner, LANES), jnp.float32)] * count
    out_shape += [jax.ShapeDtypeStruct((parts, per, 4 * EDGE * dates, LANES), jnp.float32)]
    if first:
        out_shape += [jax.ShapeDtypeStruct((RADIUS, dates, cols), jnp.float32)] * 2
        out_shape += [jax.ShapeDtypeStruct((cols // LANES, dates, 2 * EDGE, LANES), jnp.float32)]
        scratch = [pltpu.VMEM((dates, rows, span), jnp.float32) for span in (width, LANES, LANES)] + [
            pltpu.VMEM((cols // LANES, dates, 2 * EDGE, LANES), jnp.float32),
            pltpu.VMEM((RADIUS, dates, cols), jnp.float32),
            pltpu.VMEM((RADIUS, dates, cols), jnp.float32),
            pltpu.SemaphoreType.DMA((2, cols // LANES)),
            pltpu.SemaphoreType.DMA((3,)),
        ]
    else:
        scratch = [pltpu.VMEM((dates, rows, cols), jnp.float32)]
    return pl.pallas_call(
        functools.partial(interior_kernel, offsets, slot, parts, group),
        grid_spec=pltpu.PrefetchScalarGridSpec(
            num_scalar_prefetch=2,
            grid=(),
            in_specs=[here] * (1 if first else 2),
            out_specs=[here] * len(out_shape),
            scratch_shapes=scratch + [
                pltpu.VMEM((count, per, dates, inner, LANES), jnp.float32),
                pltpu.VMEM((count, per, 4 * EDGE * dates, LANES), jnp.float32),
                pltpu.VMEM((12 * LANES, width), jnp.bfloat16),
                pltpu.VMEM((inner, 4 * rows), jnp.bfloat16),
                pltpu.SemaphoreType.DMA((3, dates // group)),
                pltpu.SemaphoreType.DMA((count, dates // group)),
                pltpu.SemaphoreType.DMA((count,)),
            ],
        ),
        out_shape=out_shape,
        input_output_aliases={} if first else {3: count},
        compiler_params=params(63),
        cost_estimate=cost(2.5 + 2.5 * count),
    )(place, taps, stack, *([] if first else [brim]))


def edge_kernel(order, feet, place, taps, *rest):
    parts = len(order)
    meta, vectors, rest = rest[:parts], rest[parts:2 * parts], rest[2 * parts:]
    ends, up, down, brim, *rest = rest
    inner, outs, rest = rest[:parts], rest[parts:2 * parts], rest[2 * parts:]
    sums_ref, across_ref, brim_ref, up_ref, down_ref, ends_ref, col_ref, x_ref, v_ref = rest[:9]
    halo_sem, brim_sem, out_sem, x_sem = rest[9:]
    _, dates, cols = up_ref.shape
    width = cols // parts
    per = width // LANES
    pitch = x_ref.shape[3]
    rows = pitch - EDGE
    owners = sums_ref.shape[0]
    halos = [
        pltpu.make_async_copy(whole, ref, halo_sem.at[n])
        for n, (whole, ref) in enumerate(((up, up_ref), (down, down_ref), (ends, ends_ref)))
    ]
    for copy in halos:
        copy.start()
    for n in range(parts):
        pltpu.make_async_copy(brim.at[n], brim_ref.at[n], brim_sem.at[n]).start()
    middles = [
        pltpu.make_async_copy(inner[n], x_ref.at[n, :, :, pl.ds(EDGE, rows - 2 * EDGE), :], x_sem.at[n]) for n in range(parts)
    ]
    for copy in middles:
        copy.start()
    fill_columns(col_ref, taps)
    total = taps[0]
    for k in range(1, 2 * RADIUS + 1):
        total = total + taps[k]
    scale = 1.0 / jnp.full((dates, LANES), total, jnp.float32)
    flat = ends_ref.reshape(cols // LANES, dates * 2 * EDGE, LANES)

    def store(n):
        return [
            pltpu.make_async_copy(
                x_ref.at[n, :, :, pl.ds(side * (rows - EDGE), EDGE), :],
                outs[n].at[:, :, pl.ds(side * EDGE, EDGE), :], out_sem.at[n, side])
            for side in range(2)
        ]

    for copy in halos:
        copy.wait()

    mids, rims = [], []
    for n in range(parts):
        block = place[0] ^ order[n]
        start = pl.multiple_of(block * width, LANES)
        before = pl.multiple_of(jnp.maximum(start - LANES, 0), LANES)
        after = pl.multiple_of(jnp.minimum(start + width, cols - LANES), LANES)

        def both(first, span):
            at = pl.ds(first, span)
            return jnp.concatenate([up_ref[:, :, at], down_ref[:, :, at]], axis=0).reshape(2 * RADIUS * dates, span)

        mids.append(both(start, width))
        rims.append(rim_tile(both(before, LANES), both(after, LANES), block, parts))
    across = filter_columns(jnp.concatenate(mids, axis=0), jnp.concatenate(rims, axis=0), col_ref[...])
    span = 2 * RADIUS * dates
    for n in range(parts):
        for h in range(per):
            across_ref[n, h] = across[n * span:(n + 1) * span, h * LANES:(h + 1) * LANES]

    def one(n, carry):
        block = place[0] ^ chosen(n, order)
        every = x_ref.at[n].reshape(per, dates * pitch, LANES)
        pltpu.make_async_copy(brim.at[n], brim_ref.at[n], brim_sem.at[n]).wait()

        def half(h, carry):
            for side in range(2):
                held = []
                for q in range(2 * RADIUS + EDGE):
                    halo = q < RADIUS if side == 0 else q >= RADIUS + EDGE
                    if halo:
                        at = q if side == 0 else q - EDGE
                        held.append(across_ref[n, h, at * dates:(at + 1) * dates, :])
                    else:
                        at = q - RADIUS if side == 0 else 3 * EDGE - RADIUS + q
                        held.append(jnp.concatenate([
                            brim_ref[n, h, (d * 4 * EDGE + at) * EDGE:(d * 4 * EDGE + at + 1) * EDGE, :]
                            for d in range(dates // EDGE)
                        ], axis=0))
                for r in range(EDGE):
                    low = taps[0] * held[r]
                    for j in range(1, 2 * RADIUS + 1):
                        low = low + taps[j] * held[r + j]
                    at = pl.ds(side * EDGE + r, dates, stride=2 * EDGE)
                    done = flat[block * per + h, at, :] - scale * low
                    every[h, pl.ds(side * (rows - EDGE) + r, dates, stride=pitch), :] = done
            return carry

        lax.fori_loop(0, per, half, 0)
        for m in range(parts):
            @pl.when(n == m)
            def _():
                for copy in store(m):
                    copy.start()
        return carry

    lax.fori_loop(0, parts, one, 0)

    lane = lax.broadcasted_iota(jnp.int32, (dates, LANES), 1)
    both = [jnp.concatenate([ref[n:n + 1, :] for ref in vectors], axis=1) for n in range(1, 4)]
    index = lax.broadcasted_iota(jnp.int32, both[0].shape, 1)
    source = (index // feet) ^ place[0]
    named = lax.broadcasted_iota(jnp.int32, (owners, index.shape[1]), 0) == both[1]
    places = []
    for block in range(parts):
        for slot in range(PAIR_CAP):
            hit = named & (source == block) & (both[2] == slot)
            places.append(jnp.where(hit, 1.0, 0.0).astype(jnp.bfloat16))
    places = jnp.concatenate(places, axis=0)
    pixel_rows = x_ref.reshape(parts * per * dates * pitch, LANES)
    for copy in middles:
        copy.wait()
    for k in range(parts):
        base = order.index(k) * per * dates * pitch

        def take(f, carry):
            pixels = pixel_rows[pl.ds(base + meta[k][0, f], dates, stride=pitch), :]
            v_ref[k * feet + f] = jnp.where(lane < meta[k][1, f], pixels, 0.0)
            return carry

        lax.fori_loop(0, feet, take, 0, unroll=8)
    tiles = []
    for first in range(0, parts * feet, LANES):

        def add(f, total):
            one = jnp.sum(v_ref[first + f], axis=1, keepdims=True)
            return jnp.where(lane == f, one, total)

        tiles.append(lax.fori_loop(0, LANES, add, jnp.zeros((dates, LANES), jnp.float32), unroll=32))
    counts = jnp.broadcast_to(both[0].astype(jnp.float32), (dates, index.shape[1]))
    sums = jnp.concatenate([jnp.concatenate(tiles, axis=1), counts], axis=0)
    held = jnp.zeros((places.shape[0], 2 * dates), jnp.float32)
    for piece in split(sums, 3):
        held = held + lax.dot_general(places, piece, (((1,), (1,)), ((), ())), preferred_element_type=jnp.float32)
    for n in range(parts * PAIR_CAP):
        at = pl.ds(n * dates, dates)
        sums_ref[:, 0, at] = held[n * owners:(n + 1) * owners, :dates]
        sums_ref[:, 1, at] = held[n * owners:(n + 1) * owners, dates:]
    for m in range(parts):
        for copy in store(m):
            copy.wait()


def edges(ends, up, down, brim, inner, meta, taps, place, order, owners):
    parts = len(order)
    tiles, dates, _, _ = ends.shape
    per = tiles // parts
    feet = meta[0].shape[1]
    rows = inner[0].shape[2] + 2 * EDGE
    here = pl.BlockSpec(memory_space=pltpu.HBM)
    resident = pl.BlockSpec(memory_space=pltpu.VMEM)
    return pl.pallas_call(
        functools.partial(edge_kernel, order, feet),
        grid_spec=pltpu.PrefetchScalarGridSpec(
            num_scalar_prefetch=2 + parts,
            grid=(),
            in_specs=[resident] * parts + [here] * (4 + parts),
            out_specs=[here] * parts + [resident],
            scratch_shapes=[
                pltpu.VMEM((parts, per, 2 * RADIUS * dates, LANES), jnp.float32),
                pltpu.VMEM((parts, per, 4 * EDGE * dates, LANES), jnp.float32),
                pltpu.VMEM(up.shape, jnp.float32),
                pltpu.VMEM(up.shape, jnp.float32),
                pltpu.VMEM(ends.shape, jnp.float32),
                pltpu.VMEM((12 * LANES, per * LANES), jnp.bfloat16),
                pltpu.VMEM((parts, per, dates, rows + EDGE, LANES), jnp.float32),
                pltpu.VMEM((parts * feet, dates, LANES), jnp.float32),
                pltpu.SemaphoreType.DMA((3,)),
                pltpu.SemaphoreType.DMA((parts,)),
                pltpu.SemaphoreType.DMA((parts, 2)),
                pltpu.SemaphoreType.DMA((parts,)),
            ],
        ),
        out_shape=[jax.ShapeDtypeStruct((per, dates, 2 * EDGE, LANES), jnp.float32)] * parts
        + [jax.ShapeDtypeStruct((owners, 2, parts * PAIR_CAP * dates), jnp.float32)],
        compiler_params=params(63),
        cost_estimate=cost(8),
    )(place, taps, *meta, *meta, ends, up, down, brim, *inner)


def temporal_kernel(parts, strips, first_tile, tile_step, place, taps, *rest):
    pieces, rest = rest[:parts], rest[parts:]
    if strips:
        _, got_ref, out, anomaly, series, anomaly_ref, series_ref, owner_sem, *rest = rest
    else:
        out, *rest = rest
    z_ref, f_ref, out_ref, in_sem, out_sem = rest
    count, total, _, _ = out_ref.shape
    per = pieces[0].shape[0]
    local = total // parts
    pad = REACH * DILATION
    step = 8

    def load(n):
        rows = pl.ds(pl.multiple_of(n * EDGE, EDGE), EDGE)
        return [
            pltpu.make_async_copy(
                pieces[k].at[:, :, rows, :],
                z_ref.at[n, :, pl.ds(REACH + (place[0] ^ k) * local, local)], in_sem.at[n, k])
            for k in range(parts)
        ]

    def store(n):
        tile = first_tile + n * tile_step
        rows = pl.ds(pl.multiple_of(tile * EDGE, EDGE), EDGE)
        return pltpu.make_async_copy(out_ref.at[n], out.at[:, rows, :], out_sem.at[n])

    for n in range(count):
        for copy in load(n):
            copy.start()
    owner_copies = []
    if strips:
        series_ref[...], anomaly_ref[0] = owner_values(parts, strips, taps, got_ref)
        owner_copies = [
            pltpu.make_async_copy(series_ref, series, owner_sem.at[0]),
            pltpu.make_async_copy(anomaly_ref, anomaly, owner_sem.at[1]),
        ]
        for copy in owner_copies:
            copy.start()
    none = jnp.zeros((REACH, EDGE, LANES), jnp.float32)
    wide = jnp.zeros((pad, EDGE, LANES), jnp.float32)
    for h in range(per):
        for n in range(count):
            z_ref[n, h, 0:REACH] = none
            z_ref[n, h, REACH + total:REACH + total + REACH] = none
        f_ref[h, 0:pad] = wide
        f_ref[h, pad + total:pad + total + pad] = wide
    own = 1.0 - taps[0, REACH]
    own_wide = 1.0 - taps[1, REACH]
    others = [k for k in range(2 * REACH + 1) if k != REACH]

    def one(n, carry):
        for copy in load(n):
            copy.wait()
        for h in range(per):
            for t in range(0, total, step):
                z = z_ref[n, h, t:t + step + 2 * REACH]
                kept = own * z[REACH:REACH + step]
                for k in others:
                    kept = kept - taps[0, k] * z[k:k + step]
                f_ref[h, pad + t:pad + t + step] = kept
            for t in range(0, total, step):
                kept = own_wide * f_ref[h, pad + t:pad + t + step]
                for k in others:
                    kept = kept - taps[1, k] * f_ref[h, t + k * DILATION:t + k * DILATION + step]
                out_ref[n, t:t + step, :, h * LANES:(h + 1) * LANES] = kept
        store(n).start()
        return carry

    lax.fori_loop(0, count, one, 0)
    for n in range(count):
        store(n).wait()
    for copy in owner_copies:
        copy.wait()


def temporal(pieces, taps, place, first_tile, tile_step, rows, base=None, got=None, strips=0):
    parts = len(pieces)
    per, local, here, _ = pieces[0].shape
    total = local * parts
    count = here // EDGE
    width = per * LANES
    anywhere = pl.BlockSpec(memory_space=pl.ANY)
    whole = pl.BlockSpec(memory_space=pltpu.HBM)
    in_specs, out_specs, scratch = [anywhere] * parts, [whole], []
    out_shape = [jax.ShapeDtypeStruct((total, rows, width), jnp.float32)]
    extra = []
    if strips:
        extra = [base, got]
        in_specs += [anywhere, pl.BlockSpec(memory_space=pltpu.VMEM)]
        out_specs += [whole] * 2
        shapes = [(1, parts * strips * PAIR_CAP, total), (1, total)]
        out_shape += [jax.ShapeDtypeStruct(shape, jnp.float32) for shape in shapes]
        scratch = [pltpu.VMEM(shape, jnp.float32) for shape in shapes] + [pltpu.SemaphoreType.DMA((2,))]
    return pl.pallas_call(
        functools.partial(temporal_kernel, parts, strips, first_tile, tile_step),
        grid_spec=pltpu.PrefetchScalarGridSpec(
            num_scalar_prefetch=2,
            grid=(),
            in_specs=in_specs,
            out_specs=out_specs,
            scratch_shapes=scratch + [
                pltpu.VMEM((count, per, total + 2 * REACH, EDGE, LANES), jnp.float32),
                pltpu.VMEM((per, total + 2 * REACH * DILATION, EDGE, LANES), jnp.float32),
                pltpu.VMEM((count, total, EDGE, width), jnp.float32),
                pltpu.SemaphoreType.DMA((count, parts)),
                pltpu.SemaphoreType.DMA((count,)),
            ],
        ),
        out_shape=out_shape,
        input_output_aliases={2 + parts: 0} if strips else {},
        compiler_params=params(24),
        cost_estimate=cost(2.5 + 0.4 * count),
    )(place, taps, *pieces, *extra)


def owner_values(parts, strips, taps, got_ref):
    owners = parts * strips
    slots = owners * PAIR_CAP
    dates = got_ref.shape[2] // PAIR_CAP
    local = dates // parts
    sums, held = got_ref[:, 0, :], got_ref[:, 1, :]
    rows, weights = [], []
    for block in range(parts):
        for slot in range(PAIR_CAP):
            at = (block * PAIR_CAP + slot) * local
            rows.append(jnp.concatenate(
                [sums[e * strips:(e + 1) * strips, at:at + local] for e in range(parts)], axis=1))
            weights.append(held[0:strips, at:at + 1])
    sums = jnp.concatenate(rows, axis=0)
    weight = jnp.concatenate(weights, axis=0)
    shape = (dates, dates)
    lag = lax.broadcasted_iota(jnp.int32, shape, 0) - lax.broadcasted_iota(jnp.int32, shape, 1)
    for level, spacing in ((0, 1), (1, DILATION)):
        filt = jnp.where(lag == 0, 1.0, 0.0)
        for k in range(2 * REACH + 1):
            filt = filt - jnp.where(lag == (k - REACH) * spacing, taps[level, k], 0.0)
        sums = jnp.dot(sums, filt, precision=HIGHEST, preferred_element_type=jnp.float32)
    mean = sums / jnp.where(weight > 0, weight, 1.0)
    asset = jnp.sum(weight * mean, axis=0, keepdims=True) / jnp.sum(weight, axis=0, keepdims=True)
    odd = jnp.where(weight > 0, mean - asset, 0.0)
    shape = (slots, slots)
    to = lax.broadcasted_iota(jnp.int32, shape, 0)
    source = lax.broadcasted_iota(jnp.int32, shape, 1)
    block, rest = source // (PAIR_CAP * strips), source % (PAIR_CAP * strips)
    place_of = block * (PAIR_CAP * strips) + (rest % strips) * PAIR_CAP + rest // strips
    order = jnp.where(to == place_of, 1.0, 0.0)
    return asset, jnp.dot(order, odd, precision=HIGHEST, preferred_element_type=jnp.float32)


def spread_meta(meta, offset, swap):
    known = sorted(meta)
    got = swap(jnp.concatenate([meta[k] for k in known], axis=1), offset)
    width = meta[0].shape[1]
    return meta | {k ^ offset: got[:, n * width:(n + 1) * width] for n, k in enumerate(known)}


def shards(stack, spatial_taps, temporal_taps, foot_tile, foot_row, foot_count, foot_owner):
    parts, strips = lax.axis_size("date"), lax.axis_size("strip")
    place = lax.axis_index("date").astype(jnp.int32)[None]
    dates, rows, cols = stack.shape
    feet = foot_row.shape[0]
    owner = foot_owner[:, 0]
    position = jnp.arange(feet, dtype=jnp.int32)
    earlier = (owner[:, None] == owner[None, :]) & (position[None, :] < position[:, None])
    slot = jnp.sum(earlier.astype(jnp.int32), axis=1)
    own = jnp.stack([foot_tile * (dates * (rows + EDGE)) + foot_row, foot_count, owner, slot])

    def swap(value, offset):
        return lax.ppermute(value, "date", [(i, i ^ offset) for i in range(parts)])

    order = (*range(2, parts), 1, 0)
    inner, far_inner = {}, {}
    lead = order[0]
    inner[lead], brim, last_rows, first_rows, ends = interior(stack, None, spatial_taps, place, (lead,), 0, parts)
    far_inner[lead] = swap(inner[lead], lead)
    up = lax.ppermute(last_rows, "strip", [(i, i + 1) for i in range(strips - 1)])
    down = lax.ppermute(first_rows, "strip", [(i + 1, i) for i in range(strips - 1)])
    own, brim = lax.optimization_barrier((own, brim))
    meta = {0: own}
    for bit in range(parts.bit_length() - 2, 0, -1):
        meta = spread_meta(meta, 1 << bit, swap)
    *made, brim = interior(stack, brim, spatial_taps, place, order[1:], 1, parts)
    for n, offset in enumerate(order[1:]):
        inner[offset] = made[n]
        if offset > 1:
            far_inner[offset] = swap(inner[offset], offset)
    known = sorted(meta)
    *held, far_inner[lead], brim = lax.optimization_barrier((*[meta[k] for k in known], far_inner[lead], brim))
    meta = spread_meta(dict(zip(known, held)), 1, swap)
    meta = [meta[k] for k in range(parts)]
    *made, sums = edges(
        ends, up, down, brim, [inner[k] for k in order], meta, spatial_taps, place, order, parts * strips)
    rim = dict(zip(order, made))
    far_inner[1] = swap(inner[1], 1)
    got = lax.all_to_all(sums, ("date", "strip"), split_axis=0, concat_axis=0, tiled=True)
    gate, *made = lax.optimization_barrier((swap(rim[1], 1), *[rim[k] for k in order[:-2]]))
    far_rim = {k: swap(made[n], k) for n, k in enumerate(order[:-2])}
    far_rim[1] = gate
    last = rows // EDGE - 1
    residual, = temporal(
        [inner[0]] + [far_inner[k] for k in range(1, parts)], temporal_taps, place, 1, 1, rows)
    got, residual = lax.optimization_barrier((got, residual))
    return temporal(
        [rim[0]] + [far_rim[k] for k in range(1, parts)], temporal_taps, place, 0, last, rows, residual, got, strips)


def solution(mesh):
    placed = (
        P("date", "strip", None),
        P(),
        P(),
        P(("date", "strip")),
        P(("date", "strip")),
        P(("date", "strip")),
        P(("date", "strip"), None),
    )
    return jax.shard_map(
        shards,
        mesh=mesh,
        in_specs=placed,
        out_specs=(
            P(None, "strip", "date"),
            P(("date", "strip"), None, None),
            P(("date", "strip"), None),
        ),
        check_vma=False,
    )
```

profile of v0, /device:TPU:0, one launch (start us, length us, event | category | flops | bytes accessed | tf_op | source)
XLA Modules:
  0.0 59.3 jit_solution(17392904942648068756)
XLA Ops:
  0.6 0.0 copy-start.5
  0.6 0.0 copy-start.7
  0.7 0.0 copy-start.8
  0.7 0.0 copy-start.6
  0.7 5.6 %shard_map.94 = (f32[2,16,48,128]{3,2,1,0:T(8,128)}, f32[4,2,512,128]{3,2,1,0:T(8,128)}, f32[6,16,1024]{2,1,0:T(8,128)}, f32[6,16,1024]{2,1,0:T(8,128)}, f32[8,16,16,128]{3,2,1,0:T(8,128)}) custom-call(s32[1]{0:T(128)} %bitcast.place, f32[13]{0:T(128)} %taps.7, f32[16,64,1024]{2,1,0:T(8,128)} %stack.19), custom_call_target="tpu_custom_call" | custom-call | bytes 18450000 | tf_op jit(solution)/shard_map/pallas_call | solution.py:249
  6.3 3.0 %collective-permute-start.1 = (f32[2,16,48,128]{3,2,1,0:T(8,128)}, f32[2,16,48,128]{3,2,1,0:T(8,128)}, u32[]{:S(2)}, u32[]{:S(2)}) collective-permute-start(f32[2,16,48,128]{3,2,1,0:T(8,128)} %get-tuple-element.30.rest_12_), channel_id=1, source_target_pairs={{0,16},{8,24},{16,0},{24,8},{1,17},{9,25},{17,1},{25,9},{2,18},{10... | collective-permute-start | bytes 2359304 | tf_op jit(solution)/shard_map/ppermute | solution.py:625
  9.4 4.2 %collective-permute-start.3 = (f32[6,16,1024]{2,1,0:T(8,128)}, f32[6,16,1024]{2,1,0:T(8,128)}, u32[]{:S(2)}, u32[]{:S(2)}) collective-permute-start(f32[6,16,1024]{2,1,0:T(8,128)} %get-tuple-element.36), channel_id=1, source_target_pairs={{0,1},{1,2},{2,3},{3,4},{4,5},{5,6},{6,7},{8,9},{9,10},{10,11},{11... | collective-permute-start | bytes 1179656 | tf_op jit(solution)/shard_map/ppermute | solution.py:632
  13.5 1.3 %collective-permute-start.4 = (f32[6,16,1024]{2,1,0:T(8,128)}, f32[6,16,1024]{2,1,0:T(8,128)}, u32[]{:S(2)}, u32[]{:S(2)}) collective-permute-start(f32[6,16,1024]{2,1,0:T(8,128)} %get-tuple-element.37), channel_id=1, source_target_pairs={{1,0},{2,1},{3,2},{4,3},{5,4},{6,5},{7,6},{9,8},{10,9},{11,10},{12... | collective-permute-start | bytes 1179656 | tf_op jit(solution)/shard_map/ppermute | solution.py:633
  14.8 0.0 copy-done.5
  14.8 0.2 convert_reduce_fusion
  15.0 0.0 copy-done.7
  15.0 0.0 copy-done.8
  15.0 0.0 copy-done.6
  15.0 0.0 copy-start.3
  15.1 0.6 collective-permute-start
  15.6 9.1 %shard_map.95 = (f32[2,16,48,128]{3,2,1,0:T(8,128)}, f32[2,16,48,128]{3,2,1,0:T(8,128)}, f32[2,16,48,128]{3,2,1,0:T(8,128)}, f32[4,2,512,128]{3,2,1,0:T(8,128)}) custom-call(s32[1]{0:T(128)} %bitcast.place, f32[13]{0:T(128)} %taps.7, f32[16,64,1024]{2,1,0:T(8,128)} %stack.19, ...), custom_call_target="tpu_custom_call", output_to_operand_aliasing={{3}: (3, {})} | custom-call | bytes 36900000 | tf_op jit(solution)/shard_map/pallas_call | solution.py:249
  24.7 0.0 copy-start
  24.7 0.0 copy-start.2
  24.8 0.2 collective-permute-start.9
  25.0 2.3 %collective-permute-done.rest_2_.rest_6_ = s32[4,32]{1,0:T(4,128)S(1)} collective-permute-done((s32[4,32]{1,0:T(4,128)S(1)}, s32[4,32]{1,0:T(4,128)S(1)}, u32[]{:S(2)}, u32[]{:S(2)}) %collective-permute-start) | collective-permute-done | bytes 544 | tf_op jit(solution)/shard_map/ppermute | solution.py:625
  27.2 0.0 copy-start.4
  27.2 0.0 collective-permute-start.8
  27.3 0.0 collective-permute-done.1.rest_2_
  27.3 0.1 pad_add_fusion.1
  27.3 0.5 collective-permute-start.2
  27.8 1.5 %collective-permute-done.2 = s32[4,64]{1,0:T(4,128)S(1)} collective-permute-done((s32[4,64]{1,0:T(4,128)S(1)}, s32[4,64]{1,0:T(4,128)S(1)}, u32[]{:S(2)}, u32[]{:S(2)}) %collective-permute-start.2) | collective-permute-done | bytes 1056 | tf_op jit(solution)/shard_map/ppermute | solution.py:625
  29.3 0.7 %fusion.1 = (s32[4,32]{1,0:T(4,128)}, s32[4,32]{1,0:T(4,128)}) fusion(s32[4,64]{1,0:T(4,128)S(1)} %collective-permute-done.2), kind=kLoop, calls=%fused_computation.6 | loop fusion | bytes 2048 | tf_op jit(solution)/shard_map/slice | solution.py:610
  30.0 0.0 collective-permute-done.3.rest_9_
  30.0 0.0 collective-permute-done.4.rest_10_
  30.0 0.0 copy-done.3
  30.0 0.0 copy-done.4
  30.0 9.2 %shard_map.96 = (f32[2,16,16,128]{3,2,1,0:T(8,128)}, f32[2,16,16,128]{3,2,1,0:T(8,128)}, f32[2,16,16,128]{3,2,1,0:T(8,128)}, f32[2,16,16,128]{3,2,1,0:T(8,128)}, f32[32,2,128]{2,1,0:T(2,128)}) custom-call(s32[1]{0:T(128)} %bitcast.place, f32[13]{0:T(128)} %taps.7, s32[4,32]{1,0:T(4,128)} %copy-done.3, s32[4,32]{1,0:T(4,128)} %get-tuple-element.54.rest_1_.rest_5_, ...), custom_call_target="tpu_custom_call" | custom-call | bytes 29520000 | tf_op jit(solution)/shard_map/pallas_call | solution.py:427
  39.2 0.0 copy-start.1
  39.2 0.3 collective-permute-start.5
  39.5 1.5 %collective-permute-done.5.rest_1_ = f32[2,16,16,128]{3,2,1,0:T(8,128)S(1)} collective-permute-done((f32[2,16,16,128]{3,2,1,0:T(8,128)}, f32[2,16,16,128]{3,2,1,0:T(8,128)S(1)}, u32[]{:S(2)}, u32[]{:S(2)}) %collective-permute-start.5) | collective-permute-done | bytes 262176 | tf_op jit(solution)/shard_map/ppermute | solution.py:625
  41.1 1.7 %collective-permute-start.6 = (f32[2,16,16,128]{3,2,1,0:T(8,128)}, f32[2,16,16,128]{3,2,1,0:T(8,128)S(1)}, u32[]{:S(2)}, u32[]{:S(2)}) collective-permute-start(f32[2,16,16,128]{3,2,1,0:T(8,128)} %get-tuple-element.47), channel_id=1, source_target_pairs={{0,16},{8,24},{16,0},{24,8},{1,17},{9,25},{17,1},{25,9},{2,18},{10... | collective-permute-start | bytes 786440 | tf_op jit(solution)/shard_map/ppermute | solution.py:625
  42.8 0.0 collective-permute-start.7
  42.8 6.1 %all-to-all-start = ((f32[32,2,128]{2,1,0:T(2,128)}), f32[32,2,128]{2,1,0:T(2,128)S(1)}, u32[]{:S(2)}, u32[]{:S(2)}) async-start(f32[32,2,128]{2,1,0:T(2,128)} %get-tuple-element.49), calls=%async_computation | async-start | bytes 65536 | tf_op jit(solution)/shard_map/all_to_all | solution.py:651
  48.9 0.0 collective-permute-done.9.rest_3_
  48.9 0.0 collective-permute-done.8.rest_1_
  48.9 0.0 copy-done
  48.9 0.0 copy-done.2
  48.9 4.6 %shard_map.97.rest_4_ = f32[64,64,256]{2,1,0:T(8,128)} custom-call(s32[1]{0:T(128)} %bitcast.place, f32[2,5]{1,0:T(2,128)S(1)} %copy-done.2, f32[2,16,48,128]{3,2,1,0:T(8,128)S(1)} %copy-done, f32[2,16,48,128]{3,2,1,0:T(8,128)} %collective-permute-done.8.rest_1_, f32[2,16,48,128]{3,2,1,0:T(8,128)} %collective-permute-done.1.rest_2_, ...), custom_call_target="tpu_custom_call" | custom-call | bytes 18081000 | tf_op jit(solution)/shard_map/pallas_call | solution.py:550
  53.6 2.9 %all-to-all-done.rest_5_ = f32[32,2,128]{2,1,0:T(2,128)S(1)} async-done(((f32[32,2,128]{2,1,0:T(2,128)}), f32[32,2,128]{2,1,0:T(2,128)S(1)}, u32[]{:S(2)}, u32[]{:S(2)}) %all-to-all-start) | async-done | bytes 32800 | tf_op jit(solution)/shard_map/all_to_all | solution.py:651
  56.5 0.0 collective-permute-done.6.rest_2_
  56.5 0.0 collective-permute-done.7.rest_3_
  56.5 0.0 copy-done.1
  56.5 2.8 %shard_map.98 = (f32[64,64,256]{2,1,0:T(8,128)}, f32[1,64,64]{2,1,0:T(8,128)}, f32[1,64]{1,0:T(1,128)}) custom-call(s32[1]{0:T(128)} %bitcast.place, f32[2,5]{1,0:T(2,128)S(1)} %copy-done.2, f32[2,16,16,128]{3,2,1,0:T(8,128)S(1)} %copy-done.1, f32[2,16,16,128]{3,2,1,0:T(8,128)S(1)} %collective-permute-done.5.rest_1_, ...), custom_call_target="tpu_custom_call", output_to_operand_aliasing={{0}: (6, {})} | custom-call | bytes 12177000 | tf_op jit(solution)/shard_map/pallas_call | solution.py:550
  (2 shorter events, 0.0 us)
Async XLA Ops:
  0.6 14.2 %copy-start.5 = (s32[32,1]{0,1:T(1,128)S(1)}, s32[32,1]{0,1:T(1,128)}, u32[]{:S(2)}) copy-start(s32[32,1]{0,1:T(1,128)} %param.13) | copy-start | bytes 388
  0.6 14.4 %copy-start.7 = (s32[32]{0:T(128)S(1)}, s32[32]{0:T(128)}, u32[]{:S(2)}) copy-start(s32[32]{0:T(128)} %param.11) | copy-start | bytes 388
  0.7 14.3 %copy-start.8 = (s32[32]{0:T(128)S(1)}, s32[32]{0:T(128)}, u32[]{:S(2)}) copy-start(s32[32]{0:T(128)} %param.10) | copy-start | bytes 388
  0.7 14.4 %copy-start.6 = (s32[32]{0:T(128)S(1)}, s32[32]{0:T(128)}, u32[]{:S(2)}) copy-start(s32[32]{0:T(128)} %param.12) | copy-start | bytes 388
  6.3 20.9 %collective-permute-start.1 = (f32[2,16,48,128]{3,2,1,0:T(8,128)}, f32[2,16,48,128]{3,2,1,0:T(8,128)}, u32[]{:S(2)}, u32[]{:S(2)}) collective-permute-start(f32[2,16,48,128]{3,2,1,0:T(8,128)} %get-tuple-element.30.rest_12_), channel_id=1, source_target_pairs={{0,16},{8,24},{16,0},{24,8},{1,17},{9,25},{17,1},{25,9},{2,18},{10... | collective-permute-start | bytes 2359304 | tf_op jit(solution)/shard_map/ppermute | solution.py:625
  9.4 20.6 %collective-permute-start.3 = (f32[6,16,1024]{2,1,0:T(8,128)}, f32[6,16,1024]{2,1,0:T(8,128)}, u32[]{:S(2)}, u32[]{:S(2)}) collective-permute-start(f32[6,16,1024]{2,1,0:T(8,128)} %get-tuple-element.36), channel_id=1, source_target_pairs={{0,1},{1,2},{2,3},{3,4},{4,5},{5,6},{6,7},{8,9},{9,10},{10,11},{11... | collective-permute-start | bytes 1179656 | tf_op jit(solution)/shard_map/ppermute | solution.py:632
  13.5 16.5 %collective-permute-start.4 = (f32[6,16,1024]{2,1,0:T(8,128)}, f32[6,16,1024]{2,1,0:T(8,128)}, u32[]{:S(2)}, u32[]{:S(2)}) collective-permute-start(f32[6,16,1024]{2,1,0:T(8,128)} %get-tuple-element.37), channel_id=1, source_target_pairs={{1,0},{2,1},{3,2},{4,3},{5,4},{6,5},{7,6},{9,8},{10,9},{11,10},{12... | collective-permute-start | bytes 1179656 | tf_op jit(solution)/shard_map/ppermute | solution.py:633
  15.0 14.9 %copy-start.3 = (s32[4,32]{1,0:T(4,128)}, s32[4,32]{1,0:T(4,128)S(1)}, u32[]{:S(2)}) copy-start(s32[4,32]{1,0:T(4,128)S(1)} %pad_add_fusion.rest_0_.rest_4_) | copy-start | bytes 1540
  15.1 12.2 %collective-permute-start = (s32[4,32]{1,0:T(4,128)S(1)}, s32[4,32]{1,0:T(4,128)S(1)}, u32[]{:S(2)}, u32[]{:S(2)}) collective-permute-start(s32[4,32]{1,0:T(4,128)S(1)} %pad_add_fusion.rest_0_.rest_4_), channel_id=1, source_target_pairs={{0,16},{8,24},{16,0},{24,8},{1,17},{9,25},{17,1},{25,9},{2,18},{10... | collective-permute-start | bytes 1544 | tf_op jit(solution)/shard_map/ppermute | solution.py:625
  24.7 24.2 %copy-start = (f32[2,16,48,128]{3,2,1,0:T(8,128)S(1)}, f32[2,16,48,128]{3,2,1,0:T(8,128)}, u32[]{:S(2)}) copy-start(f32[2,16,48,128]{3,2,1,0:T(8,128)} %get-tuple-element.41.rest_15_.rest_0_) | copy-start | bytes 2359300
  24.7 24.2 %copy-start.2 = (f32[2,5]{1,0:T(2,128)S(1)}, f32[2,5]{1,0:T(2,128)}, u32[]{:S(2)}) copy-start(f32[2,5]{1,0:T(2,128)} %taps.9) | copy-start | bytes 124
  24.8 24.1 %collective-permute-start.9 = (f32[2,16,48,128]{3,2,1,0:T(8,128)}, f32[2,16,48,128]{3,2,1,0:T(8,128)}, u32[]{:S(2)}, u32[]{:S(2)}) collective-permute-start(f32[2,16,48,128]{3,2,1,0:T(8,128)} %get-tuple-element.39.rest_13_), channel_id=1, source_target_pairs={{0,24},{8,16},{16,8},{24,0},{1,25},{9,17},{17,9},{25,1},{2,26},{10... | collective-permute-start | bytes 2359304 | tf_op jit(solution)/shard_map/ppermute | solution.py:625
  27.2 2.7 %copy-start.4 = (s32[4,32]{1,0:T(4,128)}, s32[4,32]{1,0:T(4,128)S(1)}, u32[]{:S(2)}) copy-start(s32[4,32]{1,0:T(4,128)S(1)} %collective-permute-done.rest_2_.rest_6_) | copy-start | bytes 1540
  27.2 21.6 %collective-permute-start.8 = (f32[2,16,48,128]{3,2,1,0:T(8,128)}, f32[2,16,48,128]{3,2,1,0:T(8,128)}, u32[]{:S(2)}, u32[]{:S(2)}) collective-permute-start(f32[2,16,48,128]{3,2,1,0:T(8,128)} %get-tuple-element.40.rest_14_), channel_id=1, source_target_pairs={{0,8},{8,0},{16,24},{24,16},{1,9},{9,1},{17,25},{25,17},{2,10},{10... | collective-permute-start | bytes 2359304 | tf_op jit(solution)/shard_map/ppermute | solution.py:625
  27.3 2.0 %collective-permute-start.2 = (s32[4,64]{1,0:T(4,128)S(1)}, s32[4,64]{1,0:T(4,128)S(1)}, u32[]{:S(2)}, u32[]{:S(2)}) collective-permute-start(s32[4,64]{1,0:T(4,128)S(1)} %pad_add_fusion.1), channel_id=1, source_target_pairs={{0,8},{8,0},{16,24},{24,16},{1,9},{9,1},{17,25},{25,17},{2,10},{10... | collective-permute-start | bytes 3080 | tf_op jit(solution)/shard_map/ppermute | solution.py:625
  39.2 17.2 %copy-start.1 = (f32[2,16,16,128]{3,2,1,0:T(8,128)S(1)}, f32[2,16,16,128]{3,2,1,0:T(8,128)}, u32[]{:S(2)}) copy-start(f32[2,16,16,128]{3,2,1,0:T(8,128)} %get-tuple-element.42.rest_0_) | copy-start | bytes 786436
  39.2 1.8 %collective-permute-start.5 = (f32[2,16,16,128]{3,2,1,0:T(8,128)}, f32[2,16,16,128]{3,2,1,0:T(8,128)S(1)}, u32[]{:S(2)}, u32[]{:S(2)}) collective-permute-start(f32[2,16,16,128]{3,2,1,0:T(8,128)} %get-tuple-element.43), channel_id=1, source_target_pairs={{0,8},{8,0},{16,24},{24,16},{1,9},{9,1},{17,25},{25,17},{2,10},{10... | collective-permute-start | bytes 786440 | tf_op jit(solution)/shard_map/ppermute | solution.py:625
  41.1 15.4 %collective-permute-start.6 = (f32[2,16,16,128]{3,2,1,0:T(8,128)}, f32[2,16,16,128]{3,2,1,0:T(8,128)S(1)}, u32[]{:S(2)}, u32[]{:S(2)}) collective-permute-start(f32[2,16,16,128]{3,2,1,0:T(8,128)} %get-tuple-element.47), channel_id=1, source_target_pairs={{0,16},{8,24},{16,0},{24,8},{1,17},{9,25},{17,1},{25,9},{2,18},{10... | collective-permute-start | bytes 786440 | tf_op jit(solution)/shard_map/ppermute | solution.py:625
  42.8 13.7 %collective-permute-start.7 = (f32[2,16,16,128]{3,2,1,0:T(8,128)}, f32[2,16,16,128]{3,2,1,0:T(8,128)S(1)}, u32[]{:S(2)}, u32[]{:S(2)}) collective-permute-start(f32[2,16,16,128]{3,2,1,0:T(8,128)} %get-tuple-element.48), channel_id=1, source_target_pairs={{0,24},{8,16},{16,8},{24,0},{1,25},{9,17},{17,9},{25,1},{2,26},{10... | collective-permute-start | bytes 786440 | tf_op jit(solution)/shard_map/ppermute | solution.py:625
  42.8 13.7 %all-to-all-start = ((f32[32,2,128]{2,1,0:T(2,128)}), f32[32,2,128]{2,1,0:T(2,128)S(1)}, u32[]{:S(2)}, u32[]{:S(2)}) async-start(f32[32,2,128]{2,1,0:T(2,128)} %get-tuple-element.49), calls=%async_computation | async-start | bytes 65536 | tf_op jit(solution)/shard_map/all_to_all | solution.py:651
where the time goes:
time: 59.6 us; the launch traced here: 59.3 us
  Pallas kernels  31.4 us (53%)
  starting transfers between devices  17.8 us (30%)
  waiting for transfers between devices  8.2 us (14%)
  between operations  0.85 us (1%)
  local copies, waits for them, and re-layouts  0.7 us (1%)
    pallas_call x2, Pallas kernels, interior(): pl.pallas_call(functools.partial(interior_kernel, offsets, slot, parts, g...  14.7 us
    pallas_call x1, Pallas kernels, edges(): pl.pallas_call(functools.partial(edge_kernel, order, feet), grid_spec=plt...  9.23 us
    pallas_call x2, Pallas kernels, temporal(): pl.pallas_call(functools.partial(temporal_kernel, parts, strips, first_ti...  7.44 us
    ppermute x8, starting transfers between devices, swap(): return lax.ppermute(value, 'date', [(i, i ^ offset) for i in range(parts)])  6.32 us
    all_to_all x1, starting transfers between devices, shards(): lax.all_to_all(sums, ('date', 'strip'), split_axis=0, concat_axis=0, tile...  6.07 us
    ppermute x8, waiting for transfers between devices, swap(): return lax.ppermute(value, 'date', [(i, i ^ offset) for i in range(parts)])  5.3 us
    ppermute x1, starting transfers between devices, shards(): lax.ppermute(last_rows, 'strip', [(i, i + 1) for i in range(strips - 1)])  4.15 us
    all_to_all x1, waiting for transfers between devices, shards(): lax.all_to_all(sums, ('date', 'strip'), split_axis=0, concat_axis=0, tile...  2.9 us
  transfers between devices with their start and end apart: 11, of which 4 were waited for; matrix products, arithmetic and copies ran while one was open for 2% of the time, Pallas kernels for 39%

commit v1 on v0

--- a/solution.py
+++ b/solution.py
@@ -18,7 +18,7 @@
 
 
 def params(mebibytes):
-    return pltpu.CompilerParams(vmem_limit_bytes=mebibytes * 1024 * 1024)
+    return pltpu.CompilerParams(vmem_limit_bytes=int(mebibytes * 1024 * 1024))
 
 
 def cost(micros):
@@ -47,17 +47,17 @@
 
 def spread(value, axis):
     high, mid = split(value, 2)
-    return jnp.concatenate([high, high, high, mid], axis=axis)
+    return jnp.concatenate([high, high, mid], axis=axis)
 
 
 def fill_columns(col_ref, taps):
     shape = (LANES, LANES)
     lag = lax.broadcasted_iota(jnp.int32, shape, 0) - lax.broadcasted_iota(jnp.int32, shape, 1)
-    near = split(pick_taps(lag + RADIUS, taps), 3)
+    near = split(pick_taps(lag + RADIUS, taps), 2)
     far = pick_taps(jnp.where(lag > 0, lag + RADIUS - LANES, lag + RADIUS + LANES), taps)
-    above = split(jnp.where(lag > 0, far, 0.0), 3)
-    below = split(jnp.where(lag > 0, 0.0, far), 3)
-    for n, piece in enumerate((0, 1, 2, 0)):
+    above = split(jnp.where(lag > 0, far, 0.0), 2)
+    below = split(jnp.where(lag > 0, 0.0, far), 2)
+    for n, piece in enumerate((0, 1, 0)):
         at = n * 3 * LANES
         for i, pair in enumerate(((near, above), (below, near), (above, below))):
             for j, block in enumerate(pair):
@@ -65,18 +65,18 @@
 
 
 def row_band(out_rows, in_rows, taps):
-    shape = (out_rows, 4 * in_rows)
+    shape = (out_rows, 3 * in_rows)
     lane = lax.broadcasted_iota(jnp.int32, shape, 1)
     row = lax.broadcasted_iota(jnp.int32, shape, 0)
     part = jnp.zeros(shape, jnp.int32)
-    for n in range(1, 4):
+    for n in range(1, 3):
         part = jnp.where(lane >= n * in_rows, n, part)
     return lane - part * in_rows, row, part
 
 
 def pieces_of(values, part):
-    high, mid, low = [p.astype(jnp.float32) for p in split(values, 3)]
-    return jnp.where(part == 1, mid, jnp.where(part == 2, low, high)).astype(jnp.bfloat16)
+    high, mid = [p.astype(jnp.float32) for p in split(values, 2)]
+    return jnp.where(part == 1, mid, high).astype(jnp.bfloat16)
 
 
 def filter_columns(mid, rim, col):
@@ -106,7 +106,7 @@
         rest = rest[1:]
     outs, brim, rest = rest[:count], rest[count], rest[count + 1:]
     if first:
-        up, down, ends, mid_ref, left_ref, right_ref, halo_ref, up_ref, down_ref, halo_sem, halo_out_sem, *rest = rest
+        up, down, mid_ref, left_ref, right_ref, halo_ref, up_ref, down_ref, halo_sem, halo_out_sem, *rest = rest
     else:
         x_ref, *rest = rest
     out_ref, brim_ref, col_ref, row_ref, in_sem, out_sem, brim_sem = rest
@@ -134,8 +134,9 @@
         at = pl.ds(g * group, group)
         return pltpu.make_async_copy(out_ref.at[m, :, at], outs[m].at[:, at], out_sem.at[m, g])
 
-    def store_brim(n):
-        return pltpu.make_async_copy(brim_ref.at[n], brim.at[slot + n], brim_sem.at[n])
+    def store_brim(n, g):
+        at = pl.ds(g * group * 4 * EDGE, group * 4 * EDGE)
+        return pltpu.make_async_copy(brim_ref.at[n, :, at], brim.at[slot + n, :, at], brim_sem.at[n, g])
 
     for g in range(steps):
         for copy in load(g):
@@ -149,9 +150,8 @@
             for side in range(2) for c in range(cols // LANES)
         ]
         halo_stores = [
-            pltpu.make_async_copy(halo_ref, ends, halo_out_sem.at[0]),
-            pltpu.make_async_copy(up_ref, up, halo_out_sem.at[1]),
-            pltpu.make_async_copy(down_ref, down, halo_out_sem.at[2]),
+            pltpu.make_async_copy(up_ref, up, halo_out_sem.at[0]),
+            pltpu.make_async_copy(down_ref, down, halo_out_sem.at[1]),
         ]
         for copy in halo_loads:
             copy.start()
@@ -208,10 +208,7 @@
             def _():
                 store(m, g).start()
 
-        @pl.when(g == steps - 1)
-        def _():
-            store_brim(n).start()
-
+        store_brim(n, g).start()
         return carry
 
     lax.fori_loop(0, count * steps, step, 0)
@@ -220,7 +217,7 @@
     for m in range(count):
         for g in range(steps):
             store(m, g).wait()
-        store_brim(m).wait()
+            store_brim(m, g).wait()
 
 
 def interior(stack, brim, taps, place, offsets, slot, parts):
@@ -236,13 +233,12 @@
     out_shape += [jax.ShapeDtypeStruct((parts, per, 4 * EDGE * dates, LANES), jnp.float32)]
     if first:
         out_shape += [jax.ShapeDtypeStruct((RADIUS, dates, cols), jnp.float32)] * 2
-        out_shape += [jax.ShapeDtypeStruct((cols // LANES, dates, 2 * EDGE, LANES), jnp.float32)]
         scratch = [pltpu.VMEM((dates, rows, span), jnp.float32) for span in (width, LANES, LANES)] + [
             pltpu.VMEM((cols // LANES, dates, 2 * EDGE, LANES), jnp.float32),
             pltpu.VMEM((RADIUS, dates, cols), jnp.float32),
             pltpu.VMEM((RADIUS, dates, cols), jnp.float32),
             pltpu.SemaphoreType.DMA((2, cols // LANES)),
-            pltpu.SemaphoreType.DMA((3,)),
+            pltpu.SemaphoreType.DMA((2,)),
         ]
     else:
         scratch = [pltpu.VMEM((dates, rows, cols), jnp.float32)]
@@ -256,16 +252,16 @@
             scratch_shapes=scratch + [
                 pltpu.VMEM((count, per, dates, inner, LANES), jnp.float32),
                 pltpu.VMEM((count, per, 4 * EDGE * dates, LANES), jnp.float32),
-                pltpu.VMEM((12 * LANES, width), jnp.bfloat16),
-                pltpu.VMEM((inner, 4 * rows), jnp.bfloat16),
+                pltpu.VMEM((9 * LANES, width), jnp.bfloat16),
+                pltpu.VMEM((inner, 3 * rows), jnp.bfloat16),
                 pltpu.SemaphoreType.DMA((3, dates // group)),
                 pltpu.SemaphoreType.DMA((count, dates // group)),
-                pltpu.SemaphoreType.DMA((count,)),
+                pltpu.SemaphoreType.DMA((count, dates // group)),
             ],
         ),
         out_shape=out_shape,
         input_output_aliases={} if first else {3: count},
-        compiler_params=params(63),
+        compiler_params=params(63.5),
         cost_estimate=cost(2.5 + 2.5 * count),
     )(place, taps, stack, *([] if first else [brim]))
 
@@ -273,10 +269,10 @@
 def edge_kernel(order, feet, place, taps, *rest):
     parts = len(order)
     meta, vectors, rest = rest[:parts], rest[parts:2 * parts], rest[2 * parts:]
-    ends, up, down, brim, *rest = rest
+    stack, up, down, brim, *rest = rest
     inner, outs, rest = rest[:parts], rest[parts:2 * parts], rest[2 * parts:]
     sums_ref, across_ref, brim_ref, up_ref, down_ref, ends_ref, col_ref, x_ref, v_ref = rest[:9]
-    halo_sem, brim_sem, out_sem, x_sem = rest[9:]
+    halo_sem, ends_sem, brim_sem, out_sem, x_sem = rest[9:]
     _, dates, cols = up_ref.shape
     width = cols // parts
     per = width // LANES
@@ -285,9 +281,15 @@
     owners = sums_ref.shape[0]
     halos = [
         pltpu.make_async_copy(whole, ref, halo_sem.at[n])
-        for n, (whole, ref) in enumerate(((up, up_ref), (down, down_ref), (ends, ends_ref)))
+        for n, (whole, ref) in enumerate(((up, up_ref), (down, down_ref)))
     ]
-    for copy in halos:
+    ends = [
+        pltpu.make_async_copy(
+            stack.at[:, pl.ds(side * (rows - EDGE), EDGE), pl.ds(c * LANES, LANES)],
+            ends_ref.at[c, :, pl.ds(side * EDGE, EDGE), :], ends_sem.at[side, c])
+        for side in range(2) for c in range(cols // LANES)
+    ]
+    for copy in halos + ends:
         copy.start()
     for n in range(parts):
         pltpu.make_async_copy(brim.at[n], brim_ref.at[n], brim_sem.at[n]).start()
@@ -332,6 +334,8 @@
     for n in range(parts):
         for h in range(per):
             across_ref[n, h] = across[n * span:(n + 1) * span, h * LANES:(h + 1) * LANES]
+    for copy in ends:
+        copy.wait()
 
     def one(n, carry):
         block = place[0] ^ chosen(n, order)
@@ -416,12 +420,12 @@
             copy.wait()
 
 
-def edges(ends, up, down, brim, inner, meta, taps, place, order, owners):
+def edges(stack, up, down, brim, inner, meta, taps, place, order, owners):
     parts = len(order)
-    tiles, dates, _, _ = ends.shape
+    dates, rows, cols = stack.shape
+    tiles = cols // LANES
     per = tiles // parts
     feet = meta[0].shape[1]
-    rows = inner[0].shape[2] + 2 * EDGE
     here = pl.BlockSpec(memory_space=pltpu.HBM)
     resident = pl.BlockSpec(memory_space=pltpu.VMEM)
     return pl.pallas_call(
@@ -436,11 +440,12 @@
                 pltpu.VMEM((parts, per, 4 * EDGE * dates, LANES), jnp.float32),
                 pltpu.VMEM(up.shape, jnp.float32),
                 pltpu.VMEM(up.shape, jnp.float32),
-                pltpu.VMEM(ends.shape, jnp.float32),
-                pltpu.VMEM((12 * LANES, per * LANES), jnp.bfloat16),
+                pltpu.VMEM((tiles, dates, 2 * EDGE, LANES), jnp.float32),
+                pltpu.VMEM((9 * LANES, per * LANES), jnp.bfloat16),
                 pltpu.VMEM((parts, per, dates, rows + EDGE, LANES), jnp.float32),
                 pltpu.VMEM((parts * feet, dates, LANES), jnp.float32),
-                pltpu.SemaphoreType.DMA((3,)),
+                pltpu.SemaphoreType.DMA((2,)),
+                pltpu.SemaphoreType.DMA((2, tiles)),
                 pltpu.SemaphoreType.DMA((parts,)),
                 pltpu.SemaphoreType.DMA((parts, 2)),
                 pltpu.SemaphoreType.DMA((parts,)),
@@ -448,9 +453,9 @@
         ),
         out_shape=[jax.ShapeDtypeStruct((per, dates, 2 * EDGE, LANES), jnp.float32)] * parts
         + [jax.ShapeDtypeStruct((owners, 2, parts * PAIR_CAP * dates), jnp.float32)],
-        compiler_params=params(63),
+        compiler_params=params(63.5),
         cost_estimate=cost(8),
-    )(place, taps, *meta, *meta, ends, up, down, brim, *inner)
+    )(place, taps, *meta, *meta, stack, up, down, brim, *inner)
 
 
 def temporal_kernel(parts, strips, first_tile, tile_step, place, taps, *rest):
@@ -627,7 +632,7 @@
     order = (*range(2, parts), 1, 0)
     inner, far_inner = {}, {}
     lead = order[0]
-    inner[lead], brim, last_rows, first_rows, ends = interior(stack, None, spatial_taps, place, (lead,), 0, parts)
+    inner[lead], brim, last_rows, first_rows = interior(stack, None, spatial_taps, place, (lead,), 0, parts)
     far_inner[lead] = swap(inner[lead], lead)
     up = lax.ppermute(last_rows, "strip", [(i, i + 1) for i in range(strips - 1)])
     down = lax.ppermute(first_rows, "strip", [(i + 1, i) for i in range(strips - 1)])
@@ -645,7 +650,7 @@
     meta = spread_meta(dict(zip(known, held)), 1, swap)
     meta = [meta[k] for k in range(parts)]
     *made, sums = edges(
-        ends, up, down, brim, [inner[k] for k in order], meta, spatial_taps, place, order, parts * strips)
+        stack, up, down, brim, [inner[k] for k in order], meta, spatial_taps, place, order, parts * strips)
     rim = dict(zip(order, made))
     far_inner[1] = swap(inner[1], 1)
     got = lax.all_to_all(sums, ("date", "strip"), split_axis=0, concat_axis=0, tiled=True)

time: 59.6 us -> 60 us (level)
  local copies, waits for them, and re-layouts: 0.7 us -> 2.54 us
  starting transfers between devices: 17.8 us -> 16.4 us
  waiting for transfers between devices: 8.2 us -> 9.6 us
  Pallas kernels: 31.4 us -> 30 us
    ppermute x8, waiting for transfers between devices: 5.3 us -> 7.7 us  [swap(): return lax.ppermute(value, 'date', [(i, i ^ offset) for i in range(parts)])]
    unnamed x18 -> x20, local copies, waits for them, and re-layouts: 0.04 us -> 1.88 us
    pallas_call x2, Pallas kernels: 14.7 us -> 13.4 us  [interior(): pl.pallas_call(functools.partial(interior_kernel, offsets, slot, parts, g...]
    all_to_all x1, waiting for transfers between devices: 2.9 us -> 1.89 us  [shards(): lax.all_to_all(sums, ('date', 'strip'), split_axis=0, concat_axis=0, tile...]
    all_to_all x1, starting transfers between devices: 6.07 us -> 5.14 us  [shards(): lax.all_to_all(sums, ('date', 'strip'), split_axis=0, concat_axis=0, tile...]
    ppermute x1, starting transfers between devices: 4.15 us -> 3.41 us  [shards(): lax.ppermute(last_rows, 'strip', [(i, i + 1) for i in range(strips - 1)])]
  transfers between devices with their start and end apart: 11 -> 11, of which waited for: 4 -> 4; matrix products, arithmetic and copies ran while one was open for 2% -> 2% of each run, Pallas kernels for 39% -> 37%
where the time goes in v1:
time: 60 us; the launch traced here: 59.6 us
  Pallas kernels  30 us (50%)
  starting transfers between devices  16.4 us (27%)
  waiting for transfers between devices  9.6 us (16%)
  local copies, waits for them, and re-layouts  2.54 us (4%)
  between operations  0.84 us (1%)
    pallas_call x2, Pallas kernels, interior(): pl.pallas_call(functools.partial(interior_kernel, offsets, slot, parts, g...  13.4 us
    pallas_call x1, Pallas kernels, edges(): pl.pallas_call(functools.partial(edge_kernel, order, feet), grid_spec=plt...  9.1 us
    ppermute x8, waiting for transfers between devices, swap(): return lax.ppermute(value, 'date', [(i, i ^ offset) for i in range(parts)])  7.7 us
    pallas_call x2, Pallas kernels, temporal(): pl.pallas_call(functools.partial(temporal_kernel, parts, strips, first_ti...  7.44 us
    ppermute x8, starting transfers between devices, swap(): return lax.ppermute(value, 'date', [(i, i ^ offset) for i in range(parts)])  6.53 us
    all_to_all x1, starting transfers between devices, shards(): lax.all_to_all(sums, ('date', 'strip'), split_axis=0, concat_axis=0, tile...  5.14 us
    ppermute x1, starting transfers between devices, shards(): lax.ppermute(last_rows, 'strip', [(i, i + 1) for i in range(strips - 1)])  3.41 us
    all_to_all x1, waiting for transfers between devices, shards(): lax.all_to_all(sums, ('date', 'strip'), split_axis=0, concat_axis=0, tile...  1.89 us
  transfers between devices with their start and end apart: 11, of which 4 were waited for; matrix products, arithmetic and copies ran while one was open for 2% of the time, Pallas kernels for 37%

profile of v1, /device:TPU:0, one launch (start us, length us, event | category | flops | bytes accessed | tf_op | source)
XLA Modules:
  0.0 59.6 jit_solution(13408077694630718666)
XLA Ops:
  0.6 0.0 copy-start.6
  0.6 0.0 copy-start.8
  0.7 0.0 copy-start.9
  0.7 0.0 copy-start.7
  0.7 5.3 %shard_map.94 = (f32[2,16,48,128]{3,2,1,0:T(8,128)}, f32[4,2,512,128]{3,2,1,0:T(8,128)}, f32[6,16,1024]{2,1,0:T(8,128)}, f32[6,16,1024]{2,1,0:T(8,128)}) custom-call(s32[1]{0:T(128)} %bitcast.place, f32[13]{0:T(128)} %taps.7, f32[16,64,1024]{2,1,0:T(8,128)} %rest_8_.1), custom_call_target="tpu_custom_call" | custom-call | bytes 18450000 | tf_op jit(solution)/shard_map/pallas_call | solution.py:245
  6.0 3.0 %collective-permute-start.1 = (f32[2,16,48,128]{3,2,1,0:T(8,128)}, f32[2,16,48,128]{3,2,1,0:T(8,128)}, u32[]{:S(2)}, u32[]{:S(2)}) collective-permute-start(f32[2,16,48,128]{3,2,1,0:T(8,128)} %get-tuple-element.29.rest_12_), channel_id=1, source_target_pairs={{0,16},{8,24},{16,0},{24,8},{1,17},{9,25},{17,1},{25,9},{2,18},{10... | collective-permute-start | bytes 2359304 | tf_op jit(solution)/shard_map/ppermute | solution.py:630
  9.0 3.4 %collective-permute-start.3 = (f32[6,16,1024]{2,1,0:T(8,128)}, f32[6,16,1024]{2,1,0:T(8,128)S(1)}, u32[]{:S(2)}, u32[]{:S(2)}) collective-permute-start(f32[6,16,1024]{2,1,0:T(8,128)} %get-tuple-element.34), channel_id=1, source_target_pairs={{0,1},{1,2},{2,3},{3,4},{4,5},{5,6},{6,7},{8,9},{9,10},{10,11},{11... | collective-permute-start | bytes 1179656 | tf_op jit(solution)/shard_map/ppermute | solution.py:637
  12.4 1.3 %collective-permute-start.4 = (f32[6,16,1024]{2,1,0:T(8,128)}, f32[6,16,1024]{2,1,0:T(8,128)}, u32[]{:S(2)}, u32[]{:S(2)}) collective-permute-start(f32[6,16,1024]{2,1,0:T(8,128)} %get-tuple-element.35), channel_id=1, source_target_pairs={{1,0},{2,1},{3,2},{4,3},{5,4},{6,5},{7,6},{9,8},{10,9},{11,10},{12... | collective-permute-start | bytes 1179656 | tf_op jit(solution)/shard_map/ppermute | solution.py:638
  13.7 0.0 copy-done.6
  13.7 0.2 convert_reduce_fusion
  13.9 0.0 copy-done.8
  13.9 0.0 copy-done.9
  13.9 0.0 copy-done.7
  14.0 0.0 copy-start.4
  14.0 0.6 collective-permute-start
  14.5 8.2 %shard_map.95 = (f32[2,16,48,128]{3,2,1,0:T(8,128)}, f32[2,16,48,128]{3,2,1,0:T(8,128)}, f32[2,16,48,128]{3,2,1,0:T(8,128)}, f32[4,2,512,128]{3,2,1,0:T(8,128)}) custom-call(s32[1]{0:T(128)} %bitcast.place, f32[13]{0:T(128)} %taps.7, f32[16,64,1024]{2,1,0:T(8,128)} %rest_8_.1, ...), custom_call_target="tpu_custom_call", output_to_operand_aliasing={{3}: (3, {})} | custom-call | bytes 36900000 | tf_op jit(solution)/shard_map/pallas_call | solution.py:245
  22.7 0.2 collective-permute-start.9
  22.9 4.7 %collective-permute-done.rest_2_.rest_6_ = s32[4,32]{1,0:T(4,128)S(1)} collective-permute-done((s32[4,32]{1,0:T(4,128)S(1)}, s32[4,32]{1,0:T(4,128)S(1)}, u32[]{:S(2)}, u32[]{:S(2)}) %collective-permute-start) | collective-permute-done | bytes 544 | tf_op jit(solution)/shard_map/ppermute | solution.py:630
  27.6 0.0 collective-permute-start.8
  27.6 0.0 collective-permute-done.1.rest_2_
  27.6 0.1 pad_add_fusion.1
  27.7 0.5 collective-permute-start.2
  28.2 1.5 %collective-permute-done.2 = s32[4,64]{1,0:T(4,128)S(1)} collective-permute-done((s32[4,64]{1,0:T(4,128)S(1)}, s32[4,64]{1,0:T(4,128)S(1)}, u32[]{:S(2)}, u32[]{:S(2)}) %collective-permute-start.2) | collective-permute-done | bytes 1056 | tf_op jit(solution)/shard_map/ppermute | solution.py:630
  29.6 0.7 %fusion.1 = (s32[4,32]{1,0:T(4,128)}, s32[4,32]{1,0:T(4,128)}) fusion(s32[4,64]{1,0:T(4,128)S(1)} %collective-permute-done.2), kind=kLoop, calls=%fused_computation.6 | loop fusion | bytes 2048 | tf_op jit(solution)/shard_map/slice | solution.py:615
  30.3 0.0 collective-permute-done.3.rest_9_
  30.3 0.0 copy-start.3
  30.3 0.0 collective-permute-done.4.rest_10_
  30.3 0.0 copy-done.4
  30.3 0.0 copy-done.5
  30.3 0.7 %copy-done.3 = f32[6,16,1024]{2,1,0:T(8,128)} copy-done((f32[6,16,1024]{2,1,0:T(8,128)}, f32[6,16,1024]{2,1,0:T(8,128)S(1)}, u32[]{:S(2)}) %copy-start.3) | copy-done | bytes 393240
  31.1 9.1 %shard_map.96 = (f32[2,16,16,128]{3,2,1,0:T(8,128)}, f32[2,16,16,128]{3,2,1,0:T(8,128)}, f32[2,16,16,128]{3,2,1,0:T(8,128)}, f32[2,16,16,128]{3,2,1,0:T(8,128)}, f32[32,2,128]{2,1,0:T(2,128)}) custom-call(s32[1]{0:T(128)} %bitcast.place, f32[13]{0:T(128)} %taps.7, s32[4,32]{1,0:T(4,128)} %copy-done.4, s32[4,32]{1,0:T(4,128)} %get-tuple-element.52.rest_1_.rest_5_, ...), custom_call_target="tpu_custom_call" | custom-call | bytes 29520000 | tf_op jit(solution)/shard_map/pallas_call | solution.py:431
  40.2 0.3 collective-permute-start.5
  40.5 1.5 %collective-permute-done.5.rest_1_ = f32[2,16,16,128]{3,2,1,0:T(8,128)S(1)} collective-permute-done((f32[2,16,16,128]{3,2,1,0:T(8,128)}, f32[2,16,16,128]{3,2,1,0:T(8,128)S(1)}, u32[]{:S(2)}, u32[]{:S(2)}) %collective-permute-start.5) | collective-permute-done | bytes 262176 | tf_op jit(solution)/shard_map/ppermute | solution.py:630
  42.0 2.0 %collective-permute-start.6 = (f32[2,16,16,128]{3,2,1,0:T(8,128)}, f32[2,16,16,128]{3,2,1,0:T(8,128)S(1)}, u32[]{:S(2)}, u32[]{:S(2)}) collective-permute-start(f32[2,16,16,128]{3,2,1,0:T(8,128)} %get-tuple-element.45), channel_id=1, source_target_pairs={{0,16},{8,24},{16,0},{24,8},{1,17},{9,25},{17,1},{25,9},{2,18},{10... | collective-permute-start | bytes 786440 | tf_op jit(solution)/shard_map/ppermute | solution.py:630
  43.9 0.0 collective-permute-start.7
  43.9 5.1 %all-to-all-start = ((f32[32,2,128]{2,1,0:T(2,128)}), f32[32,2,128]{2,1,0:T(2,128)S(1)}, u32[]{:S(2)}, u32[]{:S(2)}) async-start(f32[32,2,128]{2,1,0:T(2,128)} %get-tuple-element.47), calls=%async_computation | async-start | bytes 65536 | tf_op jit(solution)/shard_map/all_to_all | solution.py:656
  49.1 0.0 collective-permute-done.9.rest_3_
  49.1 0.0 collective-permute-done.8.rest_1_
  49.1 0.0 copy-done.2
  49.1 0.0 copy-start
  49.1 1.1 %copy-done = f32[2,16,48,128]{3,2,1,0:T(8,128)S(1)} copy-done((f32[2,16,48,128]{3,2,1,0:T(8,128)S(1)}, f32[2,16,48,128]{3,2,1,0:T(8,128)}, u32[]{:S(2)}) %copy-start) | copy-done | bytes 786456
  50.3 0.0 copy-start.1
  50.3 4.6 %shard_map.97.rest_4_ = f32[64,64,256]{2,1,0:T(8,128)} custom-call(s32[1]{0:T(128)} %bitcast.place, f32[2,5]{1,0:T(2,128)S(1)} %copy-done.2, f32[2,16,48,128]{3,2,1,0:T(8,128)S(1)} %copy-done, f32[2,16,48,128]{3,2,1,0:T(8,128)} %collective-permute-done.8.rest_1_, f32[2,16,48,128]{3,2,1,0:T(8,128)} %collective-permute-done.1.rest_2_, ...), custom_call_target="tpu_custom_call" | custom-call | bytes 18081000 | tf_op jit(solution)/shard_map/pallas_call | solution.py:555
  54.9 1.9 %all-to-all-done.rest_5_ = f32[32,2,128]{2,1,0:T(2,128)S(1)} async-done(((f32[32,2,128]{2,1,0:T(2,128)}), f32[32,2,128]{2,1,0:T(2,128)S(1)}, u32[]{:S(2)}, u32[]{:S(2)}) %all-to-all-start) | async-done | bytes 32800 | tf_op jit(solution)/shard_map/all_to_all | solution.py:656
  56.8 0.0 collective-permute-done.6.rest_2_
  56.8 0.0 collective-permute-done.7.rest_3_
  56.8 0.0 copy-done.1
  56.8 2.8 %shard_map.98 = (f32[64,64,256]{2,1,0:T(8,128)}, f32[1,64,64]{2,1,0:T(8,128)}, f32[1,64]{1,0:T(1,128)}) custom-call(s32[1]{0:T(128)} %bitcast.place, f32[2,5]{1,0:T(2,128)S(1)} %copy-done.2, f32[2,16,16,128]{3,2,1,0:T(8,128)S(1)} %copy-done.1, f32[2,16,16,128]{3,2,1,0:T(8,128)S(1)} %collective-permute-done.5.rest_1_, ...), custom_call_target="tpu_custom_call", output_to_operand_aliasing={{0}: (6, {})} | custom-call | bytes 12177000 | tf_op jit(solution)/shard_map/pallas_call | solution.py:555
  (4 shorter events, 0.0 us)
Async XLA Ops:
  0.6 13.1 %copy-start.6 = (s32[32,1]{0,1:T(1,128)S(1)}, s32[32,1]{0,1:T(1,128)}, u32[]{:S(2)}) copy-start(s32[32,1]{0,1:T(1,128)} %param.13) | copy-start | bytes 388
  0.6 13.3 %copy-start.8 = (s32[32]{0:T(128)S(1)}, s32[32]{0:T(128)}, u32[]{:S(2)}) copy-start(s32[32]{0:T(128)} %param.11) | copy-start | bytes 388
  0.7 13.3 %copy-start.9 = (s32[32]{0:T(128)S(1)}, s32[32]{0:T(128)}, u32[]{:S(2)}) copy-start(s32[32]{0:T(128)} %param.10) | copy-start | bytes 388
  0.7 13.3 %copy-start.7 = (s32[32]{0:T(128)S(1)}, s32[32]{0:T(128)}, u32[]{:S(2)}) copy-start(s32[32]{0:T(128)} %param.12) | copy-start | bytes 388
  6.0 21.6 %collective-permute-start.1 = (f32[2,16,48,128]{3,2,1,0:T(8,128)}, f32[2,16,48,128]{3,2,1,0:T(8,128)}, u32[]{:S(2)}, u32[]{:S(2)}) collective-permute-start(f32[2,16,48,128]{3,2,1,0:T(8,128)} %get-tuple-element.29.rest_12_), channel_id=1, source_target_pairs={{0,16},{8,24},{16,0},{24,8},{1,17},{9,25},{17,1},{25,9},{2,18},{10... | collective-permute-start | bytes 2359304 | tf_op jit(solution)/shard_map/ppermute | solution.py:630
  9.0 21.3 %collective-permute-start.3 = (f32[6,16,1024]{2,1,0:T(8,128)}, f32[6,16,1024]{2,1,0:T(8,128)S(1)}, u32[]{:S(2)}, u32[]{:S(2)}) collective-permute-start(f32[6,16,1024]{2,1,0:T(8,128)} %get-tuple-element.34), channel_id=1, source_target_pairs={{0,1},{1,2},{2,3},{3,4},{4,5},{5,6},{6,7},{8,9},{9,10},{10,11},{11... | collective-permute-start | bytes 1179656 | tf_op jit(solution)/shard_map/ppermute | solution.py:637
  12.4 17.9 %collective-permute-start.4 = (f32[6,16,1024]{2,1,0:T(8,128)}, f32[6,16,1024]{2,1,0:T(8,128)}, u32[]{:S(2)}, u32[]{:S(2)}) collective-permute-start(f32[6,16,1024]{2,1,0:T(8,128)} %get-tuple-element.35), channel_id=1, source_target_pairs={{1,0},{2,1},{3,2},{4,3},{5,4},{6,5},{7,6},{9,8},{10,9},{11,10},{12... | collective-permute-start | bytes 1179656 | tf_op jit(solution)/shard_map/ppermute | solution.py:638
  14.0 16.4 %copy-start.4 = (s32[4,32]{1,0:T(4,128)}, s32[4,32]{1,0:T(4,128)S(1)}, u32[]{:S(2)}) copy-start(s32[4,32]{1,0:T(4,128)S(1)} %pad_add_fusion.rest_0_.rest_4_) | copy-start | bytes 1540
  14.0 13.6 %collective-permute-start = (s32[4,32]{1,0:T(4,128)S(1)}, s32[4,32]{1,0:T(4,128)S(1)}, u32[]{:S(2)}, u32[]{:S(2)}) collective-permute-start(s32[4,32]{1,0:T(4,128)S(1)} %pad_add_fusion.rest_0_.rest_4_), channel_id=1, source_target_pairs={{0,16},{8,24},{16,0},{24,8},{1,17},{9,25},{17,1},{25,9},{2,18},{10... | collective-permute-start | bytes 1544 | tf_op jit(solution)/shard_map/ppermute | solution.py:630
  22.7 26.4 %collective-permute-start.9 = (f32[2,16,48,128]{3,2,1,0:T(8,128)}, f32[2,16,48,128]{3,2,1,0:T(8,128)}, u32[]{:S(2)}, u32[]{:S(2)}) collective-permute-start(f32[2,16,48,128]{3,2,1,0:T(8,128)} %get-tuple-element.37.rest_13_), channel_id=1, source_target_pairs={{0,24},{8,16},{16,8},{24,0},{1,25},{9,17},{17,9},{25,1},{2,26},{10... | collective-permute-start | bytes 2359304 | tf_op jit(solution)/shard_map/ppermute | solution.py:630
  27.6 2.8 %copy-start.5 = (s32[4,32]{1,0:T(4,128)}, s32[4,32]{1,0:T(4,128)S(1)}, u32[]{:S(2)}) copy-start(s32[4,32]{1,0:T(4,128)S(1)} %collective-permute-done.rest_2_.rest_6_) | copy-start | bytes 1540
  27.6 21.5 %collective-permute-start.8 = (f32[2,16,48,128]{3,2,1,0:T(8,128)}, f32[2,16,48,128]{3,2,1,0:T(8,128)}, u32[]{:S(2)}, u32[]{:S(2)}) collective-permute-start(f32[2,16,48,128]{3,2,1,0:T(8,128)} %get-tuple-element.38.rest_14_), channel_id=1, source_target_pairs={{0,8},{8,0},{16,24},{24,16},{1,9},{9,1},{17,25},{25,17},{2,10},{10... | collective-permute-start | bytes 2359304 | tf_op jit(solution)/shard_map/ppermute | solution.py:630
  27.7 2.0 %collective-permute-start.2 = (s32[4,64]{1,0:T(4,128)S(1)}, s32[4,64]{1,0:T(4,128)S(1)}, u32[]{:S(2)}, u32[]{:S(2)}) collective-permute-start(s32[4,64]{1,0:T(4,128)S(1)} %pad_add_fusion.1), channel_id=1, source_target_pairs={{0,8},{8,0},{16,24},{24,16},{1,9},{9,1},{17,25},{25,17},{2,10},{10... | collective-permute-start | bytes 3080 | tf_op jit(solution)/shard_map/ppermute | solution.py:630
  30.3 0.7 %copy-start.3 = (f32[6,16,1024]{2,1,0:T(8,128)}, f32[6,16,1024]{2,1,0:T(8,128)S(1)}, u32[]{:S(2)}) copy-start(f32[6,16,1024]{2,1,0:T(8,128)S(1)} %collective-permute-done.3.rest_9_) | copy-start | bytes 1179652
  31.1 18.1 %copy-start.2 = (f32[2,5]{1,0:T(2,128)S(1)}, f32[2,5]{1,0:T(2,128)}, u32[]{:S(2)}) copy-start(f32[2,5]{1,0:T(2,128)} %taps.9) | copy-start | bytes 124
  40.2 1.8 %collective-permute-start.5 = (f32[2,16,16,128]{3,2,1,0:T(8,128)}, f32[2,16,16,128]{3,2,1,0:T(8,128)S(1)}, u32[]{:S(2)}, u32[]{:S(2)}) collective-permute-start(f32[2,16,16,128]{3,2,1,0:T(8,128)} %get-tuple-element.41), channel_id=1, source_target_pairs={{0,8},{8,0},{16,24},{24,16},{1,9},{9,1},{17,25},{25,17},{2,10},{10... | collective-permute-start | bytes 786440 | tf_op jit(solution)/shard_map/ppermute | solution.py:630
  42.0 14.8 %collective-permute-start.6 = (f32[2,16,16,128]{3,2,1,0:T(8,128)}, f32[2,16,16,128]{3,2,1,0:T(8,128)S(1)}, u32[]{:S(2)}, u32[]{:S(2)}) collective-permute-start(f32[2,16,16,128]{3,2,1,0:T(8,128)} %get-tuple-element.45), channel_id=1, source_target_pairs={{0,16},{8,24},{16,0},{24,8},{1,17},{9,25},{17,1},{25,9},{2,18},{10... | collective-permute-start | bytes 786440 | tf_op jit(solution)/shard_map/ppermute | solution.py:630
  43.9 12.9 %collective-permute-start.7 = (f32[2,16,16,128]{3,2,1,0:T(8,128)}, f32[2,16,16,128]{3,2,1,0:T(8,128)S(1)}, u32[]{:S(2)}, u32[]{:S(2)}) collective-permute-start(f32[2,16,16,128]{3,2,1,0:T(8,128)} %get-tuple-element.46), channel_id=1, source_target_pairs={{0,24},{8,16},{16,8},{24,0},{1,25},{9,17},{17,9},{25,1},{2,26},{10... | collective-permute-start | bytes 786440 | tf_op jit(solution)/shard_map/ppermute | solution.py:630
  43.9 12.9 %all-to-all-start = ((f32[32,2,128]{2,1,0:T(2,128)}), f32[32,2,128]{2,1,0:T(2,128)S(1)}, u32[]{:S(2)}, u32[]{:S(2)}) async-start(f32[32,2,128]{2,1,0:T(2,128)} %get-tuple-element.47), calls=%async_computation | async-start | bytes 65536 | tf_op jit(solution)/shard_map/all_to_all | solution.py:656
  49.1 1.1 %copy-start = (f32[2,16,48,128]{3,2,1,0:T(8,128)S(1)}, f32[2,16,48,128]{3,2,1,0:T(8,128)}, u32[]{:S(2)}) copy-start(f32[2,16,48,128]{3,2,1,0:T(8,128)} %get-tuple-element.39.rest_15_.rest_0_) | copy-start | bytes 2359300
  50.3 6.5 %copy-start.1 = (f32[2,16,16,128]{3,2,1,0:T(8,128)S(1)}, f32[2,16,16,128]{3,2,1,0:T(8,128)}, u32[]{:S(2)}) copy-start(f32[2,16,16,128]{3,2,1,0:T(8,128)} %get-tuple-element.40.rest_0_) | copy-start | bytes 786436

commit v2 on v0

--- a/solution.py
+++ b/solution.py
@@ -475,10 +475,11 @@
             for k in range(parts)
         ]
 
-    def store(n):
+    def store(n, h):
         tile = first_tile + n * tile_step
         rows = pl.ds(pl.multiple_of(tile * EDGE, EDGE), EDGE)
-        return pltpu.make_async_copy(out_ref.at[n], out.at[:, rows, :], out_sem.at[n])
+        lanes = pl.ds(h * LANES, LANES)
+        return pltpu.make_async_copy(out_ref.at[n, :, :, lanes], out.at[:, rows, lanes], out_sem.at[n, h])
 
     for n in range(count):
         for copy in load(n):
@@ -519,12 +520,13 @@
                 for k in others:
                     kept = kept - taps[1, k] * f_ref[h, t + k * DILATION:t + k * DILATION + step]
                 out_ref[n, t:t + step, :, h * LANES:(h + 1) * LANES] = kept
-        store(n).start()
+            store(n, h).start()
         return carry
 
     lax.fori_loop(0, count, one, 0)
     for n in range(count):
-        store(n).wait()
+        for h in range(per):
+            store(n, h).wait()
     for copy in owner_copies:
         copy.wait()
 
@@ -559,7 +561,7 @@
                 pltpu.VMEM((per, total + 2 * REACH * DILATION, EDGE, LANES), jnp.float32),
                 pltpu.VMEM((count, total, EDGE, width), jnp.float32),
                 pltpu.SemaphoreType.DMA((count, parts)),
-                pltpu.SemaphoreType.DMA((count,)),
+                pltpu.SemaphoreType.DMA((count, per)),
             ],
         ),
         out_shape=out_shape,

time: 59.6 us -> 59.5 us (level)
  no operation moved by 1% of the time
where the time goes in v2:
time: 59.5 us; the launch traced here: 59.2 us
  Pallas kernels  31.3 us (53%)
  starting transfers between devices  17.8 us (30%)
  waiting for transfers between devices  8.24 us (14%)
  between operations  0.85 us (1%)
  local copies, waits for them, and re-layouts  0.7 us (1%)
    pallas_call x2, Pallas kernels, interior(): pl.pallas_call(functools.partial(interior_kernel, offsets, slot, parts, g...  14.7 us
    pallas_call x1, Pallas kernels, edges(): pl.pallas_call(functools.partial(edge_kernel, order, feet), grid_spec=plt...  9.23 us
    pallas_call x2, Pallas kernels, temporal(): pl.pallas_call(functools.partial(temporal_kernel, parts, strips, first_ti...  7.33 us
    ppermute x8, starting transfers between devices, swap(): return lax.ppermute(value, 'date', [(i, i ^ offset) for i in range(parts)])  6.32 us
    all_to_all x1, starting transfers between devices, shards(): lax.all_to_all(sums, ('date', 'strip'), split_axis=0, concat_axis=0, tile...  6.07 us
    ppermute x8, waiting for transfers between devices, swap(): return lax.ppermute(value, 'date', [(i, i ^ offset) for i in range(parts)])  5.3 us
    ppermute x1, starting transfers between devices, shards(): lax.ppermute(last_rows, 'strip', [(i, i + 1) for i in range(strips - 1)])  4.15 us
    all_to_all x1, waiting for transfers between devices, shards(): lax.all_to_all(sums, ('date', 'strip'), split_axis=0, concat_axis=0, tile...  2.93 us
  transfers between devices with their start and end apart: 11, of which 4 were waited for; matrix products, arithmetic and copies ran while one was open for 2% of the time, Pallas kernels for 39%

profile of v2, /device:TPU:0, one launch (start us, length us, event | category | flops | bytes accessed | tf_op | source)
XLA Modules:
  0.0 59.2 jit_solution(1704696540009877280)
XLA Ops:
  0.6 0.0 copy-start.5
  0.6 0.0 copy-start.7
  0.7 0.0 copy-start.8
  0.7 0.0 copy-start.6
  0.7 5.6 %shard_map.94 = (f32[2,16,48,128]{3,2,1,0:T(8,128)}, f32[4,2,512,128]{3,2,1,0:T(8,128)}, f32[6,16,1024]{2,1,0:T(8,128)}, f32[6,16,1024]{2,1,0:T(8,128)}, f32[8,16,16,128]{3,2,1,0:T(8,128)}) custom-call(s32[1]{0:T(128)} %bitcast.place, f32[13]{0:T(128)} %taps.7, f32[16,64,1024]{2,1,0:T(8,128)} %stack.19), custom_call_target="tpu_custom_call" | custom-call | bytes 18450000 | tf_op jit(solution)/shard_map/pallas_call | solution.py:249
  6.3 3.0 %collective-permute-start.1 = (f32[2,16,48,128]{3,2,1,0:T(8,128)}, f32[2,16,48,128]{3,2,1,0:T(8,128)}, u32[]{:S(2)}, u32[]{:S(2)}) collective-permute-start(f32[2,16,48,128]{3,2,1,0:T(8,128)} %get-tuple-element.30.rest_12_), channel_id=1, source_target_pairs={{0,16},{8,24},{16,0},{24,8},{1,17},{9,25},{17,1},{25,9},{2,18},{10... | collective-permute-start | bytes 2359304 | tf_op jit(solution)/shard_map/ppermute | solution.py:627
  9.4 4.2 %collective-permute-start.3 = (f32[6,16,1024]{2,1,0:T(8,128)}, f32[6,16,1024]{2,1,0:T(8,128)}, u32[]{:S(2)}, u32[]{:S(2)}) collective-permute-start(f32[6,16,1024]{2,1,0:T(8,128)} %get-tuple-element.36), channel_id=1, source_target_pairs={{0,1},{1,2},{2,3},{3,4},{4,5},{5,6},{6,7},{8,9},{9,10},{10,11},{11... | collective-permute-start | bytes 1179656 | tf_op jit(solution)/shard_map/ppermute | solution.py:634
  13.5 1.3 %collective-permute-start.4 = (f32[6,16,1024]{2,1,0:T(8,128)}, f32[6,16,1024]{2,1,0:T(8,128)}, u32[]{:S(2)}, u32[]{:S(2)}) collective-permute-start(f32[6,16,1024]{2,1,0:T(8,128)} %get-tuple-element.37), channel_id=1, source_target_pairs={{1,0},{2,1},{3,2},{4,3},{5,4},{6,5},{7,6},{9,8},{10,9},{11,10},{12... | collective-permute-start | bytes 1179656 | tf_op jit(solution)/shard_map/ppermute | solution.py:635
  14.8 0.0 copy-done.5
  14.8 0.2 convert_reduce_fusion
  15.0 0.0 copy-done.7
  15.0 0.0 copy-done.8
  15.0 0.0 copy-done.6
  15.0 0.0 copy-start.3
  15.1 0.6 collective-permute-start
  15.6 9.1 %shard_map.95 = (f32[2,16,48,128]{3,2,1,0:T(8,128)}, f32[2,16,48,128]{3,2,1,0:T(8,128)}, f32[2,16,48,128]{3,2,1,0:T(8,128)}, f32[4,2,512,128]{3,2,1,0:T(8,128)}) custom-call(s32[1]{0:T(128)} %bitcast.place, f32[13]{0:T(128)} %taps.7, f32[16,64,1024]{2,1,0:T(8,128)} %stack.19, ...), custom_call_target="tpu_custom_call", output_to_operand_aliasing={{3}: (3, {})} | custom-call | bytes 36900000 | tf_op jit(solution)/shard_map/pallas_call | solution.py:249
  24.7 0.0 copy-start
  24.7 0.0 copy-start.2
  24.8 0.2 collective-permute-start.9
  25.0 2.3 %collective-permute-done.rest_2_.rest_6_ = s32[4,32]{1,0:T(4,128)S(1)} collective-permute-done((s32[4,32]{1,0:T(4,128)S(1)}, s32[4,32]{1,0:T(4,128)S(1)}, u32[]{:S(2)}, u32[]{:S(2)}) %collective-permute-start) | collective-permute-done | bytes 544 | tf_op jit(solution)/shard_map/ppermute | solution.py:627
  27.2 0.0 copy-start.4
  27.2 0.0 collective-permute-start.8
  27.3 0.0 collective-permute-done.1.rest_2_
  27.3 0.1 pad_add_fusion.1
  27.3 0.5 collective-permute-start.2
  27.8 1.5 %collective-permute-done.2 = s32[4,64]{1,0:T(4,128)S(1)} collective-permute-done((s32[4,64]{1,0:T(4,128)S(1)}, s32[4,64]{1,0:T(4,128)S(1)}, u32[]{:S(2)}, u32[]{:S(2)}) %collective-permute-start.2) | collective-permute-done | bytes 1056 | tf_op jit(solution)/shard_map/ppermute | solution.py:627
  29.3 0.7 %fusion.1 = (s32[4,32]{1,0:T(4,128)}, s32[4,32]{1,0:T(4,128)}) fusion(s32[4,64]{1,0:T(4,128)S(1)} %collective-permute-done.2), kind=kLoop, calls=%fused_computation.6 | loop fusion | bytes 2048 | tf_op jit(solution)/shard_map/slice | solution.py:612
  30.0 0.0 collective-permute-done.3.rest_9_
  30.0 0.0 collective-permute-done.4.rest_10_
  30.0 0.0 copy-done.3
  30.0 0.0 copy-done.4
  30.0 9.2 %shard_map.96 = (f32[2,16,16,128]{3,2,1,0:T(8,128)}, f32[2,16,16,128]{3,2,1,0:T(8,128)}, f32[2,16,16,128]{3,2,1,0:T(8,128)}, f32[2,16,16,128]{3,2,1,0:T(8,128)}, f32[32,2,128]{2,1,0:T(2,128)}) custom-call(s32[1]{0:T(128)} %bitcast.place, f32[13]{0:T(128)} %taps.7, s32[4,32]{1,0:T(4,128)} %copy-done.3, s32[4,32]{1,0:T(4,128)} %get-tuple-element.54.rest_1_.rest_5_, ...), custom_call_target="tpu_custom_call" | custom-call | bytes 29520000 | tf_op jit(solution)/shard_map/pallas_call | solution.py:427
  39.2 0.0 copy-start.1
  39.2 0.3 collective-permute-start.5
  39.5 1.5 %collective-permute-done.5.rest_1_ = f32[2,16,16,128]{3,2,1,0:T(8,128)S(1)} collective-permute-done((f32[2,16,16,128]{3,2,1,0:T(8,128)}, f32[2,16,16,128]{3,2,1,0:T(8,128)S(1)}, u32[]{:S(2)}, u32[]{:S(2)}) %collective-permute-start.5) | collective-permute-done | bytes 262176 | tf_op jit(solution)/shard_map/ppermute | solution.py:627
  41.1 1.7 %collective-permute-start.6 = (f32[2,16,16,128]{3,2,1,0:T(8,128)}, f32[2,16,16,128]{3,2,1,0:T(8,128)S(1)}, u32[]{:S(2)}, u32[]{:S(2)}) collective-permute-start(f32[2,16,16,128]{3,2,1,0:T(8,128)} %get-tuple-element.47), channel_id=1, source_target_pairs={{0,16},{8,24},{16,0},{24,8},{1,17},{9,25},{17,1},{25,9},{2,18},{10... | collective-permute-start | bytes 786440 | tf_op jit(solution)/shard_map/ppermute | solution.py:627
  42.8 0.0 collective-permute-start.7
  42.8 6.1 %all-to-all-start = ((f32[32,2,128]{2,1,0:T(2,128)}), f32[32,2,128]{2,1,0:T(2,128)S(1)}, u32[]{:S(2)}, u32[]{:S(2)}) async-start(f32[32,2,128]{2,1,0:T(2,128)} %get-tuple-element.49), calls=%async_computation | async-start | bytes 65536 | tf_op jit(solution)/shard_map/all_to_all | solution.py:653
  48.9 0.0 collective-permute-done.9.rest_3_
  48.9 0.0 collective-permute-done.8.rest_1_
  48.9 0.0 copy-done
  48.9 0.0 copy-done.2
  48.9 4.6 %shard_map.97.rest_4_ = f32[64,64,256]{2,1,0:T(8,128)} custom-call(s32[1]{0:T(128)} %bitcast.place, f32[2,5]{1,0:T(2,128)S(1)} %copy-done.2, f32[2,16,48,128]{3,2,1,0:T(8,128)S(1)} %copy-done, f32[2,16,48,128]{3,2,1,0:T(8,128)} %collective-permute-done.8.rest_1_, f32[2,16,48,128]{3,2,1,0:T(8,128)} %collective-permute-done.1.rest_2_, ...), custom_call_target="tpu_custom_call" | custom-call | bytes 18081000 | tf_op jit(solution)/shard_map/pallas_call | solution.py:552
  53.5 2.9 %all-to-all-done.rest_5_ = f32[32,2,128]{2,1,0:T(2,128)S(1)} async-done(((f32[32,2,128]{2,1,0:T(2,128)}), f32[32,2,128]{2,1,0:T(2,128)S(1)}, u32[]{:S(2)}, u32[]{:S(2)}) %all-to-all-start) | async-done | bytes 32800 | tf_op jit(solution)/shard_map/all_to_all | solution.py:653
  56.5 0.0 collective-permute-done.6.rest_2_
  56.5 0.0 collective-permute-done.7.rest_3_
  56.5 0.0 copy-done.1
  56.5 2.7 %shard_map.98 = (f32[64,64,256]{2,1,0:T(8,128)}, f32[1,64,64]{2,1,0:T(8,128)}, f32[1,64]{1,0:T(1,128)}) custom-call(s32[1]{0:T(128)} %bitcast.place, f32[2,5]{1,0:T(2,128)S(1)} %copy-done.2, f32[2,16,16,128]{3,2,1,0:T(8,128)S(1)} %copy-done.1, f32[2,16,16,128]{3,2,1,0:T(8,128)S(1)} %collective-permute-done.5.rest_1_, ...), custom_call_target="tpu_custom_call", output_to_operand_aliasing={{0}: (6, {})} | custom-call | bytes 12177000 | tf_op jit(solution)/shard_map/pallas_call | solution.py:552
  (2 shorter events, 0.0 us)
Async XLA Ops:
  0.6 14.2 %copy-start.5 = (s32[32,1]{0,1:T(1,128)S(1)}, s32[32,1]{0,1:T(1,128)}, u32[]{:S(2)}) copy-start(s32[32,1]{0,1:T(1,128)} %param.13) | copy-start | bytes 388
  0.6 14.4 %copy-start.7 = (s32[32]{0:T(128)S(1)}, s32[32]{0:T(128)}, u32[]{:S(2)}) copy-start(s32[32]{0:T(128)} %param.11) | copy-start | bytes 388
  0.7 14.3 %copy-start.8 = (s32[32]{0:T(128)S(1)}, s32[32]{0:T(128)}, u32[]{:S(2)}) copy-start(s32[32]{0:T(128)} %param.10) | copy-start | bytes 388
  0.7 14.4 %copy-start.6 = (s32[32]{0:T(128)S(1)}, s32[32]{0:T(128)}, u32[]{:S(2)}) copy-start(s32[32]{0:T(128)} %param.12) | copy-start | bytes 388
  6.3 20.9 %collective-permute-start.1 = (f32[2,16,48,128]{3,2,1,0:T(8,128)}, f32[2,16,48,128]{3,2,1,0:T(8,128)}, u32[]{:S(2)}, u32[]{:S(2)}) collective-permute-start(f32[2,16,48,128]{3,2,1,0:T(8,128)} %get-tuple-element.30.rest_12_), channel_id=1, source_target_pairs={{0,16},{8,24},{16,0},{24,8},{1,17},{9,25},{17,1},{25,9},{2,18},{10... | collective-permute-start | bytes 2359304 | tf_op jit(solution)/shard_map/ppermute | solution.py:627
  9.4 20.6 %collective-permute-start.3 = (f32[6,16,1024]{2,1,0:T(8,128)}, f32[6,16,1024]{2,1,0:T(8,128)}, u32[]{:S(2)}, u32[]{:S(2)}) collective-permute-start(f32[6,16,1024]{2,1,0:T(8,128)} %get-tuple-element.36), channel_id=1, source_target_pairs={{0,1},{1,2},{2,3},{3,4},{4,5},{5,6},{6,7},{8,9},{9,10},{10,11},{11... | collective-permute-start | bytes 1179656 | tf_op jit(solution)/shard_map/ppermute | solution.py:634
  13.5 16.5 %collective-permute-start.4 = (f32[6,16,1024]{2,1,0:T(8,128)}, f32[6,16,1024]{2,1,0:T(8,128)}, u32[]{:S(2)}, u32[]{:S(2)}) collective-permute-start(f32[6,16,1024]{2,1,0:T(8,128)} %get-tuple-element.37), channel_id=1, source_target_pairs={{1,0},{2,1},{3,2},{4,3},{5,4},{6,5},{7,6},{9,8},{10,9},{11,10},{12... | collective-permute-start | bytes 1179656 | tf_op jit(solution)/shard_map/ppermute | solution.py:635
  15.0 14.9 %copy-start.3 = (s32[4,32]{1,0:T(4,128)}, s32[4,32]{1,0:T(4,128)S(1)}, u32[]{:S(2)}) copy-start(s32[4,32]{1,0:T(4,128)S(1)} %pad_add_fusion.rest_0_.rest_4_) | copy-start | bytes 1540
  15.1 12.2 %collective-permute-start = (s32[4,32]{1,0:T(4,128)S(1)}, s32[4,32]{1,0:T(4,128)S(1)}, u32[]{:S(2)}, u32[]{:S(2)}) collective-permute-start(s32[4,32]{1,0:T(4,128)S(1)} %pad_add_fusion.rest_0_.rest_4_), channel_id=1, source_target_pairs={{0,16},{8,24},{16,0},{24,8},{1,17},{9,25},{17,1},{25,9},{2,18},{10... | collective-permute-start | bytes 1544 | tf_op jit(solution)/shard_map/ppermute | solution.py:627
  24.7 24.2 %copy-start = (f32[2,16,48,128]{3,2,1,0:T(8,128)S(1)}, f32[2,16,48,128]{3,2,1,0:T(8,128)}, u32[]{:S(2)}) copy-start(f32[2,16,48,128]{3,2,1,0:T(8,128)} %get-tuple-element.41.rest_15_.rest_0_) | copy-start | bytes 2359300
  24.7 24.2 %copy-start.2 = (f32[2,5]{1,0:T(2,128)S(1)}, f32[2,5]{1,0:T(2,128)}, u32[]{:S(2)}) copy-start(f32[2,5]{1,0:T(2,128)} %taps.9) | copy-start | bytes 124
  24.8 24.1 %collective-permute-start.9 = (f32[2,16,48,128]{3,2,1,0:T(8,128)}, f32[2,16,48,128]{3,2,1,0:T(8,128)}, u32[]{:S(2)}, u32[]{:S(2)}) collective-permute-start(f32[2,16,48,128]{3,2,1,0:T(8,128)} %get-tuple-element.39.rest_13_), channel_id=1, source_target_pairs={{0,24},{8,16},{16,8},{24,0},{1,25},{9,17},{17,9},{25,1},{2,26},{10... | collective-permute-start | bytes 2359304 | tf_op jit(solution)/shard_map/ppermute | solution.py:627
  27.2 2.7 %copy-start.4 = (s32[4,32]{1,0:T(4,128)}, s32[4,32]{1,0:T(4,128)S(1)}, u32[]{:S(2)}) copy-start(s32[4,32]{1,0:T(4,128)S(1)} %collective-permute-done.rest_2_.rest_6_) | copy-start | bytes 1540
  27.2 21.6 %collective-permute-start.8 = (f32[2,16,48,128]{3,2,1,0:T(8,128)}, f32[2,16,48,128]{3,2,1,0:T(8,128)}, u32[]{:S(2)}, u32[]{:S(2)}) collective-permute-start(f32[2,16,48,128]{3,2,1,0:T(8,128)} %get-tuple-element.40.rest_14_), channel_id=1, source_target_pairs={{0,8},{8,0},{16,24},{24,16},{1,9},{9,1},{17,25},{25,17},{2,10},{10... | collective-permute-start | bytes 2359304 | tf_op jit(solution)/shard_map/ppermute | solution.py:627
  27.3 2.0 %collective-permute-start.2 = (s32[4,64]{1,0:T(4,128)S(1)}, s32[4,64]{1,0:T(4,128)S(1)}, u32[]{:S(2)}, u32[]{:S(2)}) collective-permute-start(s32[4,64]{1,0:T(4,128)S(1)} %pad_add_fusion.1), channel_id=1, source_target_pairs={{0,8},{8,0},{16,24},{24,16},{1,9},{9,1},{17,25},{25,17},{2,10},{10... | collective-permute-start | bytes 3080 | tf_op jit(solution)/shard_map/ppermute | solution.py:627
  39.2 17.2 %copy-start.1 = (f32[2,16,16,128]{3,2,1,0:T(8,128)S(1)}, f32[2,16,16,128]{3,2,1,0:T(8,128)}, u32[]{:S(2)}) copy-start(f32[2,16,16,128]{3,2,1,0:T(8,128)} %get-tuple-element.42.rest_0_) | copy-start | bytes 786436
  39.2 1.8 %collective-permute-start.5 = (f32[2,16,16,128]{3,2,1,0:T(8,128)}, f32[2,16,16,128]{3,2,1,0:T(8,128)S(1)}, u32[]{:S(2)}, u32[]{:S(2)}) collective-permute-start(f32[2,16,16,128]{3,2,1,0:T(8,128)} %get-tuple-element.43), channel_id=1, source_target_pairs={{0,8},{8,0},{16,24},{24,16},{1,9},{9,1},{17,25},{25,17},{2,10},{10... | collective-permute-start | bytes 786440 | tf_op jit(solution)/shard_map/ppermute | solution.py:627
  41.1 15.4 %collective-permute-start.6 = (f32[2,16,16,128]{3,2,1,0:T(8,128)}, f32[2,16,16,128]{3,2,1,0:T(8,128)S(1)}, u32[]{:S(2)}, u32[]{:S(2)}) collective-permute-start(f32[2,16,16,128]{3,2,1,0:T(8,128)} %get-tuple-element.47), channel_id=1, source_target_pairs={{0,16},{8,24},{16,0},{24,8},{1,17},{9,25},{17,1},{25,9},{2,18},{10... | collective-permute-start | bytes 786440 | tf_op jit(solution)/shard_map/ppermute | solution.py:627
  42.8 13.7 %collective-permute-start.7 = (f32[2,16,16,128]{3,2,1,0:T(8,128)}, f32[2,16,16,128]{3,2,1,0:T(8,128)S(1)}, u32[]{:S(2)}, u32[]{:S(2)}) collective-permute-start(f32[2,16,16,128]{3,2,1,0:T(8,128)} %get-tuple-element.48), channel_id=1, source_target_pairs={{0,24},{8,16},{16,8},{24,0},{1,25},{9,17},{17,9},{25,1},{2,26},{10... | collective-permute-start | bytes 786440 | tf_op jit(solution)/shard_map/ppermute | solution.py:627
  42.8 13.7 %all-to-all-start = ((f32[32,2,128]{2,1,0:T(2,128)}), f32[32,2,128]{2,1,0:T(2,128)S(1)}, u32[]{:S(2)}, u32[]{:S(2)}) async-start(f32[32,2,128]{2,1,0:T(2,128)} %get-tuple-element.49), calls=%async_computation | async-start | bytes 65536 | tf_op jit(solution)/shard_map/all_to_all | solution.py:653
